TPU v7x, 256 devices: a whole 4x4x8 slice. The times are simulated.
256 devices in a mesh: section: 8 (over z), expert: 8 (over x, y_hi), dp: 4 (over y_lo, core).
Axes of the slice: x: 4, y: 4 (y_hi: 2, y_lo: 2; y = y_hi * 2 + y_lo), z: 8, core: 2. Of those that a mesh axis runs over, the one named last changes fastest.
Arguments:
- hidden: bfloat16 [8, 4096, 1024], P('section', ('expert', 'dp')), may hold values from -6 to 6
- expert_ids: int32 [8, 4096, 2], P('section', ('expert', 'dp')), may hold values from 0 to 7, all different within a row; in each aligned block of 128 rows (0 to 127, 128 to 255, ..., all dimensions but the last counted through in order) at most 48 rows name the same one
- cotangent: bfloat16 [8, 4096, 1024], P('section', ('expert', 'dp')), may hold values from -6 to 6
- skip_weight: bfloat16 [8, 2048, 1024], P('section'), may hold values from -0.125 to 0.125
- norm_gain: float32 [8, 1024], P('section'), may hold values from 0.25 to 1.75
- router_weight: bfloat16 [8, 1024, 8], P('section'), may hold values from -0.1875 to 0.1875
- gate_weight: bfloat16 [8, 8, 1024, 1024], P('section', 'expert'), may hold values from -0.1875 to 0.1875
- up_weight: bfloat16 [8, 8, 1024, 1024], P('section', 'expert'), may hold values from -0.1875 to 0.1875
- down_weight: bfloat16 [8, 8, 1024, 1024], P('section', 'expert'), may hold values from -0.1875 to 0.1875
Outputs:
- section_out: bfloat16 [8, 4096, 1024], P('section', ('expert', 'dp'))
- hidden_grad: bfloat16 [8, 4096, 1024], P('section', ('expert', 'dp'))
- skip_grad: float32 [8, 2048, 1024], P('section', ('expert', 'dp'))
- router_grad: float32 [8, 1024, 8], P('section')
- gain_grad: float32 [8, 1024], P('section')
Inputs may be any that keep to these rules, and one draw needn't show every extreme that they name: `expert_ids`: in the rows of one device (aligned blocks of 128 frames of each section) no expert is named more than 48 times; the two experts of a frame differ.
All inputs are finite; a program needn't handle non-finite values.
Results may differ from a plain program's by a relative error of at most 0.029.
Values may be sent and summed in bfloat16 or wider, within the bound.
A program may use at most 128 MiB of HBM per device.

v0:
```python
import jax
import jax.numpy as jnp
from jax import lax
from jax.sharding import PartitionSpec as P

norm_eps = 1e-06


def partner_2(value, axis, distance):
    mask = 2**distance
    pairs = [(source, source ^ mask) for source in range(lax.axis_size(axis))]
    return lax.ppermute(value, axis, pairs)


def matmul(left, right):
    return jnp.dot(left, right, preferred_element_type=jnp.float32)


def matmul_right_t(left, right):
    return lax.dot_general(
        left, right, (((1,), (1,)), ((), ())), preferred_element_type=jnp.float32
    )


def inner_rows(left, right):
    return lax.dot_general(
        left, right, (((0,), (0,)), ((), ())), preferred_element_type=jnp.float32
    )


def dispatch_index(expert_ids, experts, capacity):
    flat_ids = expert_ids.reshape(-1)
    expert_names = jnp.arange(experts, dtype=jnp.int32)
    onehot = (flat_ids[:, None] == expert_names[None, :]).astype(jnp.int32)
    before = jnp.cumsum(onehot, axis=0) - onehot
    return flat_ids * capacity + jnp.sum(before * onehot, axis=1)


def place_rows(row_block, target, slot_total):
    width = row_block.shape[-1]
    return jnp.zeros((slot_total, width), row_block.dtype).at[target].set(row_block)


def section_front(own_rows, partner, expert_ids, skip_weight, norm_gain, router_weight, capacity):
    experts = router_weight.shape[1]
    joined = jnp.concatenate([own_rows, partner], axis=1)
    wide_rows = matmul(joined, skip_weight).astype(jnp.bfloat16).astype(jnp.float32)
    inv_rms = lax.rsqrt(jnp.mean(wide_rows * wide_rows, axis=1, keepdims=True) + norm_eps)
    normed = (wide_rows * inv_rms * norm_gain[None, :]).astype(jnp.bfloat16)
    logits = matmul(normed, router_weight)
    expert_names = jnp.arange(experts, dtype=jnp.int32)
    chosen = (expert_ids[:, :, None] == expert_names[None, None, :]).astype(jnp.float32)
    picked = jnp.sum(chosen * logits[:, None, :], axis=2)
    scores = jax.nn.sigmoid(picked)
    weights = scores / jnp.sum(scores, axis=1, keepdims=True)
    target = dispatch_index(expert_ids, experts, capacity)
    return (joined, wide_rows, inv_rms, normed, chosen, scores, weights, target)


def expert_forward(row_block, w_gate, w_up, w_down):
    gate_pre = matmul(row_block, w_gate)
    up_pre = matmul(row_block, w_up)
    act = (jax.nn.silu(gate_pre) * up_pre).astype(jnp.bfloat16)
    return (matmul(act, w_down).astype(jnp.bfloat16), gate_pre, up_pre)


def expert_backward(grad_rows, gate_pre, up_pre, w_gate, w_up, w_down):
    grad_act = matmul_right_t(grad_rows, w_down)
    sigmoid_gate = jax.nn.sigmoid(gate_pre)
    grad_gate = (grad_act * up_pre * sigmoid_gate * (1.0 + gate_pre * (1.0 - sigmoid_gate))).astype(
        jnp.bfloat16
    )
    grad_up = (grad_act * gate_pre * sigmoid_gate).astype(jnp.bfloat16)
    return (matmul_right_t(grad_gate, w_gate) + matmul_right_t(grad_up, w_up)).astype(jnp.bfloat16)


def section_back(
    grad_out,
    picked_out,
    weights,
    scores,
    chosen,
    grad_picked,
    normed,
    wide_rows,
    inv_rms,
    norm_gain,
    router_weight,
    skip_weight,
):
    picked_wide = picked_out.astype(jnp.float32)
    grad_weight = jnp.sum(grad_out[:, None, :] * picked_wide, axis=2)
    weighted_sum = jnp.sum(weights * grad_weight, axis=1, keepdims=True)
    grad_score = (grad_weight - weighted_sum) / jnp.sum(scores, axis=1, keepdims=True)
    grad_picked_logit = grad_score * scores * (1.0 - scores)
    grad_logits = jnp.sum(chosen * grad_picked_logit[:, :, None], axis=1).astype(jnp.bfloat16)
    router_term = inner_rows(normed, grad_logits)
    grad_normed = jnp.sum(grad_picked.astype(jnp.float32), axis=1) + matmul_right_t(
        grad_logits, router_weight
    )
    unit_rows = wide_rows * inv_rms
    gain_term = jnp.sum(grad_normed * unit_rows, axis=0)
    grad_unit = grad_normed * norm_gain[None, :]
    grad_mixed = (
        grad_out
        + inv_rms * (grad_unit - unit_rows * jnp.mean(grad_unit * unit_rows, axis=1, keepdims=True))
    ).astype(jnp.bfloat16)
    grad_joined = matmul_right_t(grad_mixed, skip_weight).astype(jnp.bfloat16)
    return (grad_mixed, router_term, gain_term, grad_joined)


def per_device(
    hidden,
    expert_ids,
    cotangent,
    skip_weight,
    norm_gain,
    router_weight,
    gate_weight,
    up_weight,
    down_weight,
):
    own_rows = hidden[0]
    tokens = own_rows.shape[0]
    model_width = own_rows.shape[1]
    experts = lax.axis_size("expert")
    capacity = min(tokens, 3 * tokens // experts)
    slot_total = experts * capacity
    section_count = lax.axis_size("section")
    section_index = lax.axis_index("section")
    upper = section_index >= section_count // 2
    partner = own_rows
    for bit_index in range(section_count.bit_length() - 1):
        partner = partner_2(partner, "section", bit_index)
    partner = jnp.where(upper, partner, jnp.zeros_like(partner))
    joined, wide_rows, inv_rms, normed, chosen, scores, weights, target = section_front(
        own_rows, partner, expert_ids[0], skip_weight[0], norm_gain[0], router_weight[0], capacity
    )
    send = place_rows(jnp.repeat(normed, 2, axis=0), target, slot_total).reshape(
        experts, capacity, model_width
    )
    arrived = lax.all_to_all(send, "expert", split_axis=0, concat_axis=0, tiled=True).reshape(
        slot_total, model_width
    )
    outputs, gate_pre, up_pre = expert_forward(
        arrived, gate_weight[0, 0], up_weight[0, 0], down_weight[0, 0]
    )
    returned = lax.all_to_all(
        outputs.reshape(experts, capacity, model_width),
        "expert",
        split_axis=0,
        concat_axis=0,
        tiled=True,
    )
    picked_out = returned.reshape(slot_total, model_width)[target].reshape(tokens, 2, model_width)
    result = (
        wide_rows + jnp.sum(weights[:, :, None] * picked_out.astype(jnp.float32), axis=1)
    ).astype(jnp.bfloat16)
    grad_out = cotangent[0].astype(jnp.float32)
    grad_sent = (
        (weights[:, :, None] * grad_out[:, None, :])
        .astype(jnp.bfloat16)
        .reshape(2 * tokens, model_width)
    )
    grad_buffer = place_rows(grad_sent, target, slot_total).reshape(experts, capacity, model_width)
    grad_arrived = lax.all_to_all(
        grad_buffer, "expert", split_axis=0, concat_axis=0, tiled=True
    ).reshape(slot_total, model_width)
    grad_inputs = expert_backward(
        grad_arrived, gate_pre, up_pre, gate_weight[0, 0], up_weight[0, 0], down_weight[0, 0]
    )
    grad_back = lax.all_to_all(
        grad_inputs.reshape(experts, capacity, model_width),
        "expert",
        split_axis=0,
        concat_axis=0,
        tiled=True,
    )
    grad_picked = grad_back.reshape(slot_total, model_width)[target].reshape(tokens, 2, model_width)
    grad_mixed, router_term, gain_term, grad_joined = section_back(
        grad_out,
        picked_out,
        weights,
        scores,
        chosen,
        grad_picked,
        normed,
        wide_rows,
        inv_rms,
        norm_gain[0],
        router_weight[0],
        skip_weight[0],
    )
    router_grad, gain_grad = lax.psum((router_term, gain_term), ("expert", "dp"))
    skip_grad = lax.psum_scatter(
        inner_rows(joined, grad_mixed), ("expert", "dp"), scatter_dimension=0, tiled=True
    )
    own_grad = grad_joined[:, :model_width]
    partner_grad = grad_joined[:, model_width:]
    mirror_grad = partner_grad
    for bit_index in range(section_count.bit_length() - 1):
        mirror_grad = partner_2(mirror_grad, "section", bit_index)
    mirror_wide = jnp.where(
        upper, jnp.zeros((tokens, model_width), jnp.float32), mirror_grad.astype(jnp.float32)
    )
    hidden_grad = (own_grad.astype(jnp.float32) + mirror_wide).astype(jnp.bfloat16)
    return (result[None], hidden_grad[None], skip_grad[None], router_grad[None], gain_grad[None])


def solution(mesh):
    return jax.shard_map(
        per_device,
        mesh=mesh,
        in_specs=(
            P("section", ("expert", "dp"), None),
            P("section", ("expert", "dp"), None),
            P("section", ("expert", "dp"), None),
            P("section", None, None),
            P("section", None),
            P("section", None, None),
            P("section", "expert", None, None),
            P("section", "expert", None, None),
            P("section", "expert", None, None),
        ),
        out_specs=(
            P("section", ("expert", "dp"), None),
            P("section", ("expert", "dp"), None),
            P("section", ("expert", "dp"), None),
            P("section", None, None),
            P("section", None),
        ),
        check_vma=False,
    )
```

profile of v0, /device:TPU:1, one launch (start us, length us, event | category | flops | bytes accessed | tf_op | source)
XLA Modules:
  0.0 302.1 jit_solution(3067606964734022535)
XLA Ops:
  7.2 2.6 collective-permute-start
  12.6 2.4 collective-permute-done
  15.0 3.9 %collective-permute-start.1 = (bf16[128,1024]{1,0:T(8,128)(2,1)}, bf16[128,1024]{1,0:T(8,128)(2,1)}, u32[]{:S(2)}, u32[]{:S(2)}) collective-permute-start(bf16[128,1024]{1,0:T(8,128)(2,1)} %collective-permute-done), channel_id=1, source_target_pairs={{0,64},{32,96},{64,0},{96,32},{128,192},{160,224},{192,128},{224,1... | collective-permute-start | bytes 786440 | tf_op jit(solution)/shard_map/ppermute | solution.py:12
  23.0 7.7 %collective-permute-done.1 = bf16[128,1024]{1,0:T(8,128)(2,1)} collective-permute-done((bf16[128,1024]{1,0:T(8,128)(2,1)}, bf16[128,1024]{1,0:T(8,128)(2,1)}, u32[]{:S(2)}, u32[]{:S(2)}) %collective-permute-start.1) | collective-permute-done | bytes 262176 | tf_op jit(solution)/shard_map/ppermute | solution.py:12
  30.6 6.4 %collective-permute-start.2 = (bf16[128,1024]{1,0:T(8,128)(2,1)}, bf16[128,1024]{1,0:T(8,128)(2,1)S(1)}, u32[]{:S(2)}, u32[]{:S(2)}) collective-permute-start(bf16[128,1024]{1,0:T(8,128)(2,1)} %collective-permute-done.1), channel_id=1, source_target_pairs={{0,128},{32,160},{64,192},{96,224},{128,0},{160,32},{192,64},{224,... | collective-permute-start | bytes 786440 | tf_op jit(solution)/shard_map/ppermute | solution.py:12
  37.1 8.8 %collective-permute-done.2 = bf16[128,1024]{1,0:T(8,128)(2,1)S(1)} collective-permute-done((bf16[128,1024]{1,0:T(8,128)(2,1)}, bf16[128,1024]{1,0:T(8,128)(2,1)S(1)}, u32[]{:S(2)}, u32[]{:S(2)}) %collective-permute-start.2) | collective-permute-done | bytes 262176 | tf_op jit(solution)/shard_map/ppermute | solution.py:12
  45.9 3.1 %multiply_reduce_fusion.4 = (f32[128]{0:T(128)S(1)}, f32[128,1024]{1,0:T(8,128)S(1)}) fusion(bf16[1,2048,1024]{2,1,0:T(8,128)(2,1)} %param.12, bf16[128,1024]{1,0:T(8,128)(2,1)S(1)} %broadcast_select_fusion, bf16[128,1024]{1,0:T(8,128)(2,1)S(1)} %bitcast.86), kind=kOutput, calls=%fused_computation.46 | convolution fusion | flops 538443648 | bytes 5243392 | tf_op jit(solution)/shard_map/dot_general | solution.py:16
  51.0 3.1 %scatter_custom_fusion = bf16[384,1024]{1,0:T(8,128)(2,1)} fusion(s32[256]{0:T(256)S(1)} %bitcast.98, bf16[256,1024]{1,0:T(8,128)(2,1)} %reshape.232, bf16[]{:T(256)} %constant.14.clone.1), kind=kCustom, calls=%fused_computation.48 | custom fusion | bytes 786944 | tf_op jit(solution)/shard_map/scatter | solution.py:41
  54.1 6.6 %all-to-all-start = ((bf16[8,48,1024]{2,1,0:T(8,128)(2,1)}), bf16[8,48,1024]{2,1,0:T(8,128)(2,1)}, u32[]{:S(2)}, u32[]{:S(2)}) async-start(bf16[8,48,1024]{2,1,0:T(8,128)(2,1)} %bitcast.84), calls=%async_computation | async-start | bytes 1572864 | tf_op jit(solution)/shard_map/all_to_all | solution.py:142
  61.8 3.3 %scatter_custom_fusion.1 = bf16[384,1024]{1,0:T(8,128)(2,1)} fusion(s32[256]{0:T(256)S(1)} %bitcast.99, f32[256,1024]{1,0:T(8,128)} %mul.180, f32[256]{0:T(256)S(1)} %reshape.210, bf16[]{:T(256)} %constant.14.clone.1), kind=kCustom, calls=%fused_computation.37 | custom fusion | flops 524288 | bytes 1836034 | tf_op jit(solution)/shard_map/scatter | solution.py:41
  65.2 5.5 %all-to-all-done = bf16[8,48,1024]{2,1,0:T(8,128)(2,1)} async-done(((bf16[8,48,1024]{2,1,0:T(8,128)(2,1)}), bf16[8,48,1024]{2,1,0:T(8,128)(2,1)}, u32[]{:S(2)}, u32[]{:S(2)}) %all-to-all-start) | async-done | bytes 786464 | tf_op jit(solution)/shard_map/all_to_all | solution.py:142
  70.7 3.5 %all-to-all-start.2 = ((bf16[8,48,1024]{2,1,0:T(8,128)(2,1)}), bf16[8,48,1024]{2,1,0:T(8,128)(2,1)S(1)}, u32[]{:S(2)}, u32[]{:S(2)}) async-start(bf16[8,48,1024]{2,1,0:T(8,128)(2,1)} %bitcast.19), calls=%async_computation.2 | async-start | bytes 1572864 | tf_op jit(solution)/shard_map/all_to_all | solution.py:166
  74.3 3.0 fusion.17
  77.3 2.7 fusion.13
  84.9 5.6 %all-to-all-start.1 = ((bf16[8,48,1024]{2,1,0:T(8,128)(2,1)}), bf16[8,48,1024]{2,1,0:T(8,128)(2,1)S(1)}, u32[]{:S(2)}, u32[]{:S(2)}) async-start(bf16[8,48,1024]{2,1,0:T(8,128)(2,1)} %bitcast.90), calls=%async_computation.1 | async-start | bytes 1572864 | tf_op jit(solution)/shard_map/all_to_all | solution.py:148
  90.5 2.3 fusion.7
  94.9 2.4 add_convert_fusion
  97.3 3.0 all-to-all-done.1
  101.2 3.6 %all-to-all-start.3 = ((bf16[8,48,1024]{2,1,0:T(8,128)(2,1)}), bf16[8,48,1024]{2,1,0:T(8,128)(2,1)S(1)}, u32[]{:S(2)}, u32[]{:S(2)}) async-start(bf16[8,48,1024]{2,1,0:T(8,128)(2,1)} %bitcast.88), calls=%async_computation.3 | async-start | bytes 1572864 | tf_op jit(solution)/shard_map/all_to_all | solution.py:172
  104.9 3.6 %gather_fusion = bf16[256,1024]{1,0:T(8,128)(2,1)} fusion(bf16[384,1024]{1,0:T(8,128)(2,1)} %bitcast.83, s32[1024]{0:T(1024)S(1)} %pad_clamp_fusion), kind=kCustom, calls=%fused_computation | custom fusion | bytes 1049600 | tf_op jit(solution)/shard_map/gather | solution.py:155
  108.5 2.7 reshape.207
  111.2 4.0 %multiply_reduce_fusion = (f32[128,2]{1,0:T(8,128)S(1)}, f32[128,1024]{1,0:T(8,128)}) fusion(f32[128,2,1024]{2,1,0:T(2,128)} %reshape.207, f32[128,1024]{1,0:T(8,128)} %copy-done.2, f32[128,2]{1,0:T(8,128)S(1)} %copy.26), kind=kLoop, calls=%fused_computation.31 | loop fusion | flops 917248 | bytes 2099200 | tf_op jit(solution)/shard_map/reduce_sum | solution.py:92
  119.5 2.7 reshape.211
  122.2 3.3 %reduce_sum.111 = f32[128,1024]{1,0:T(8,128)} reduce(f32[128,2,1024]{2,1,0:T(2,128)} %reshape.211, f32[]{:T(128)} %constant.10.clone.1), dimensions={1}, to_apply=%region_9.10 | reduce | flops 131072 | bytes 1572868 | tf_op jit(solution)/shard_map/reduce_sum | solution.py:98
  128.1 4.5 %fusion.38 = f32[2048,1024]{1,0:T(8,128)} fusion(bf16[128,1024]{1,0:T(8,128)(2,1)S(1)} %get-tuple-element.13, bf16[128,1024]{1,0:T(8,128)(2,1)S(1)} %copy-done.6, bf16[128,1024]{1,0:T(8,128)(2,1)S(1)} %bitcast.87), kind=kOutput, calls=%fused_computation.50 | convolution fusion | flops 537919488 | bytes 9175040 | tf_op jit(solution)/shard_map/dot_general | solution.py:26
  132.6 3.7 %fusion.4 = bf16[128,2048]{1,0:T(8,128)(2,1)S(1)} fusion(bf16[128,1024]{1,0:T(8,128)(2,1)S(1)} %get-tuple-element.13, bf16[1,2048,1024]{2,1,0:T(8,128)(2,1)} %param.12), kind=kOutput, calls=%fused_computation.8 | convolution fusion | flops 537133056 | bytes 4980736 | tf_op jit(solution)/shard_map/dot_general | solution.py:20
  136.4 6.7 %collective-permute-start.3 = (bf16[128,1024]{1,0:T(8,128)(2,1)S(1)}, bf16[128,1024]{1,0:T(8,128)(2,1)S(1)}, u32[]{:S(2)}, u32[]{:S(2)}) collective-permute-start(bf16[128,1024]{1,0:T(8,128)(2,1)S(1)} %slice.22), channel_id=1, source_target_pairs={{0,32},{32,0},{64,96},{96,64},{128,160},{160,128},{192,224},{224,1... | collective-permute-start | bytes 786440 | tf_op jit(solution)/shard_map/ppermute | solution.py:12
  143.0 4.1 %collective-permute-done.3 = bf16[128,1024]{1,0:T(8,128)(2,1)S(1)} collective-permute-done((bf16[128,1024]{1,0:T(8,128)(2,1)S(1)}, bf16[128,1024]{1,0:T(8,128)(2,1)S(1)}, u32[]{:S(2)}, u32[]{:S(2)}) %collective-permute-start.3) | collective-permute-done | bytes 262176 | tf_op jit(solution)/shard_map/ppermute | solution.py:12
  147.1 8.9 %collective-permute-start.4 = (bf16[128,1024]{1,0:T(8,128)(2,1)S(1)}, bf16[128,1024]{1,0:T(8,128)(2,1)S(1)}, u32[]{:S(2)}, u32[]{:S(2)}) collective-permute-start(bf16[128,1024]{1,0:T(8,128)(2,1)S(1)} %collective-permute-done.3), channel_id=1, source_target_pairs={{0,64},{32,96},{64,0},{96,32},{128,192},{160,224},{192,128},{224,1... | collective-permute-start | bytes 786440 | tf_op jit(solution)/shard_map/ppermute | solution.py:12
  156.1 11.4 %collective-permute-done.4 = bf16[128,1024]{1,0:T(8,128)(2,1)S(1)} collective-permute-done((bf16[128,1024]{1,0:T(8,128)(2,1)S(1)}, bf16[128,1024]{1,0:T(8,128)(2,1)S(1)}, u32[]{:S(2)}, u32[]{:S(2)}) %collective-permute-start.4) | collective-permute-done | bytes 262176 | tf_op jit(solution)/shard_map/ppermute | solution.py:12
  167.5 2.9 collective-permute-start.5
  170.6 123.8 %all-reduce = (f32[1,1024,8]{1,2,0:T(8,128)}, f32[1,1024]{1,0:T(1,128)}) all-reduce(f32[1,1024,8]{1,2,0:T(8,128)S(1)} %convolution_bitcast_fusion, f32[1,1024]{1,0:T(1,128)S(1)} %bitcast.94), channel_id=1, replica_groups=mesh['section'=8,'expert'=8,'dp'=4] {'expert','dp'}, use_global_device_ids=true, to_apply=%region_15.16 | all-reduce | flops 9216 | bytes 73728 | tf_op jit(solution)/shard_map/psum | solution.py:194
  (103 shorter events, 25.5 us)
Async XLA Ops:
  7.2 73.9 %copy-start = (bf16[1,1,1024,1024]{3,2,1,0:T(8,128)(2,1)S(1)}, bf16[1,1,1024,1024]{3,2,1,0:T(8,128)(2,1)}, u32[]{:S(2)}) copy-start(bf16[1,1,1024,1024]{3,2,1,0:T(8,128)(2,1)} %param.17) | copy-start | bytes 6291460
  7.2 7.8 %collective-permute-start = (bf16[128,1024]{1,0:T(8,128)(2,1)}, bf16[128,1024]{1,0:T(8,128)(2,1)}, u32[]{:S(2)}, u32[]{:S(2)}) collective-permute-start(bf16[128,1024]{1,0:T(8,128)(2,1)} %bitcast.85), channel_id=1, source_target_pairs={{0,32},{32,0},{64,96},{96,64},{128,160},{160,128},{192,224},{224,1... | collective-permute-start | bytes 786440 | tf_op jit(solution)/shard_map/ppermute | solution.py:12
  15.0 15.6 %collective-permute-start.1 = (bf16[128,1024]{1,0:T(8,128)(2,1)}, bf16[128,1024]{1,0:T(8,128)(2,1)}, u32[]{:S(2)}, u32[]{:S(2)}) collective-permute-start(bf16[128,1024]{1,0:T(8,128)(2,1)} %collective-permute-done), channel_id=1, source_target_pairs={{0,64},{32,96},{64,0},{96,32},{128,192},{160,224},{192,128},{224,1... | collective-permute-start | bytes 786440 | tf_op jit(solution)/shard_map/ppermute | solution.py:12
  21.1 24.7 %copy-start.9 = (bf16[1,128,1024]{2,1,0:T(8,128)(2,1)S(1)}, bf16[1,128,1024]{2,1,0:T(8,128)(2,1)}, u32[]{:S(2)}) copy-start(bf16[1,128,1024]{2,1,0:T(8,128)(2,1)} %param.9) | copy-start | bytes 786436
  30.6 15.2 %collective-permute-start.2 = (bf16[128,1024]{1,0:T(8,128)(2,1)}, bf16[128,1024]{1,0:T(8,128)(2,1)S(1)}, u32[]{:S(2)}, u32[]{:S(2)}) collective-permute-start(bf16[128,1024]{1,0:T(8,128)(2,1)} %collective-permute-done.1), channel_id=1, source_target_pairs={{0,128},{32,160},{64,192},{96,224},{128,0},{160,32},{192,64},{224,... | collective-permute-start | bytes 786440 | tf_op jit(solution)/shard_map/ppermute | solution.py:12
  37.1 67.8 %copy-start.17 = (s32[1024]{0:T(1024)}, s32[1024]{0:T(1024)S(1)}, u32[]{:S(2)}) copy-start(s32[1024]{0:T(1024)S(1)} %pad_clamp_fusion) | copy-start | bytes 12292
  45.9 3.1 %copy-start.5 = (bf16[128,1024]{1,0:T(8,128)(2,1)}, bf16[128,1024]{1,0:T(8,128)(2,1)S(1)}, u32[]{:S(2)}) copy-start(bf16[128,1024]{1,0:T(8,128)(2,1)S(1)} %broadcast_select_fusion) | copy-start | bytes 786436
  45.9 3.7 %copy-start.13 = (f32[1,1024]{1,0:T(1,128)S(1)}, f32[1,1024]{1,0:T(1,128)}, u32[]{:S(2)}) copy-start(f32[1,1024]{1,0:T(1,128)} %param.13) | copy-start | bytes 12292
  49.7 11.1 %copy-start.3 = (bf16[128,1024]{1,0:T(8,128)(2,1)}, bf16[128,1024]{1,0:T(8,128)(2,1)S(1)}, u32[]{:S(2)}) copy-start(bf16[128,1024]{1,0:T(8,128)(2,1)S(1)} %multiply_convert_fusion.8) | copy-start | bytes 786436
  50.0 10.8 %copy-start.12 = (bf16[1,1024,8]{1,2,0:T(8,128)(2,1)S(1)}, bf16[1,1024,8]{1,2,0:T(8,128)(2,1)}, u32[]{:S(2)}) copy-start(bf16[1,1024,8]{1,2,0:T(8,128)(2,1)} %param.14) | copy-start | bytes 49156
  51.0 9.9 %copy-start.15 = (s32[1,128,2]{1,2,0:T(2,128)S(1)}, s32[1,128,2]{1,2,0:T(2,128)}, u32[]{:S(2)}) copy-start(s32[1,128,2]{1,2,0:T(2,128)} %param.10) | copy-start | bytes 3076
  54.1 16.6 %all-to-all-start = ((bf16[8,48,1024]{2,1,0:T(8,128)(2,1)}), bf16[8,48,1024]{2,1,0:T(8,128)(2,1)}, u32[]{:S(2)}, u32[]{:S(2)}) async-start(bf16[8,48,1024]{2,1,0:T(8,128)(2,1)} %bitcast.84), calls=%async_computation | async-start | bytes 1572864 | tf_op jit(solution)/shard_map/all_to_all | solution.py:142
  61.0 9.7 %copy-start.16 = (f32[128,2]{0,1:T(2,128)}, f32[128,2]{0,1:T(2,128)S(1)}, u32[]{:S(2)}) copy-start(f32[128,2]{0,1:T(2,128)S(1)} %select_reduce_fusion.1) | copy-start | bytes 3076
  61.6 9.1 %copy-start.18 = (f32[128]{0:T(128)}, f32[128]{0:T(128)S(1)}, u32[]{:S(2)}) copy-start(f32[128]{0:T(128)S(1)} %get-tuple-element.11) | copy-start | bytes 1540
  70.7 13.3 %all-to-all-start.2 = ((bf16[8,48,1024]{2,1,0:T(8,128)(2,1)}), bf16[8,48,1024]{2,1,0:T(8,128)(2,1)S(1)}, u32[]{:S(2)}, u32[]{:S(2)}) async-start(bf16[8,48,1024]{2,1,0:T(8,128)(2,1)} %bitcast.19), calls=%async_computation.2 | async-start | bytes 1572864 | tf_op jit(solution)/shard_map/all_to_all | solution.py:166
  74.3 3.0 copy-start.21
  77.3 2.7 copy-start.24
  84.9 15.4 %all-to-all-start.1 = ((bf16[8,48,1024]{2,1,0:T(8,128)(2,1)}), bf16[8,48,1024]{2,1,0:T(8,128)(2,1)S(1)}, u32[]{:S(2)}, u32[]{:S(2)}) async-start(bf16[8,48,1024]{2,1,0:T(8,128)(2,1)} %bitcast.90), calls=%async_computation.1 | async-start | bytes 1572864 | tf_op jit(solution)/shard_map/all_to_all | solution.py:148
  90.5 2.3 copy-start.22
  90.5 2.3 copy-start.25
  92.9 1.6 copy-start.23
  92.9 2.0 copy-start.27
  101.2 16.2 %all-to-all-start.3 = ((bf16[8,48,1024]{2,1,0:T(8,128)(2,1)}), bf16[8,48,1024]{2,1,0:T(8,128)(2,1)S(1)}, u32[]{:S(2)}, u32[]{:S(2)}) async-start(bf16[8,48,1024]{2,1,0:T(8,128)(2,1)} %bitcast.88), calls=%async_computation.3 | async-start | bytes 1572864 | tf_op jit(solution)/shard_map/all_to_all | solution.py:172
  104.8 190.4 %reduce-scatter.2.cloned.1.call-start = ((), (), s32[]{:S(2)}) async-start(), calls=%async_computation.5 | async-start | bytes 8650752 | tf_op jit(solution)/shard_map/reduce_scatter | solution.py:195
  119.5 6.0 %copy-start.14 = (f32[1,1024]{1,0:T(1,128)S(1)}, f32[1,1024]{1,0:T(1,128)}, u32[]{:S(2)}) copy-start(f32[1,1024]{1,0:T(1,128)} %param.13) | copy-start | bytes 12292
  119.5 6.0 %copy-start.20 = (f32[128]{0:T(128)S(1)}, f32[128]{0:T(128)}, u32[]{:S(2)}) copy-start(f32[128]{0:T(128)} %copy-done.19) | copy-start | bytes 1540
  122.2 4.9 %copy-start.7 = (f32[128,1024]{1,0:T(8,128)S(1)}, f32[128,1024]{1,0:T(8,128)}, u32[]{:S(2)}) copy-start(f32[128,1024]{1,0:T(8,128)} %get-tuple-element.8) | copy-start | bytes 1572868
  125.5 1.5 copy-start.8
  132.6 37.8 %copy-start.4 = (bf16[128,1024]{1,0:T(8,128)(2,1)S(1)}, bf16[128,1024]{1,0:T(8,128)(2,1)}, u32[]{:S(2)}) copy-start(bf16[128,1024]{1,0:T(8,128)(2,1)} %copy-done.3) | copy-start | bytes 786436
  136.4 10.8 %collective-permute-start.3 = (bf16[128,1024]{1,0:T(8,128)(2,1)S(1)}, bf16[128,1024]{1,0:T(8,128)(2,1)S(1)}, u32[]{:S(2)}, u32[]{:S(2)}) collective-permute-start(bf16[128,1024]{1,0:T(8,128)(2,1)S(1)} %slice.22), channel_id=1, source_target_pairs={{0,32},{32,0},{64,96},{96,64},{128,160},{160,128},{192,224},{224,1... | collective-permute-start | bytes 786440 | tf_op jit(solution)/shard_map/ppermute | solution.py:12
  147.1 20.4 %collective-permute-start.4 = (bf16[128,1024]{1,0:T(8,128)(2,1)S(1)}, bf16[128,1024]{1,0:T(8,128)(2,1)S(1)}, u32[]{:S(2)}, u32[]{:S(2)}) collective-permute-start(bf16[128,1024]{1,0:T(8,128)(2,1)S(1)} %collective-permute-done.3), channel_id=1, source_target_pairs={{0,64},{32,96},{64,0},{96,32},{128,192},{160,224},{192,128},{224,1... | collective-permute-start | bytes 786440 | tf_op jit(solution)/shard_map/ppermute | solution.py:12
  167.5 126.9 %collective-permute-start.5 = (bf16[128,1024]{1,0:T(8,128)(2,1)S(1)}, bf16[128,1024]{1,0:T(8,128)(2,1)S(1)}, u32[]{:S(2)}, u32[]{:S(2)}) collective-permute-start(bf16[128,1024]{1,0:T(8,128)(2,1)S(1)} %collective-permute-done.4), channel_id=1, source_target_pairs={{0,128},{32,160},{64,192},{96,224},{128,0},{160,32},{192,64},{224,... | collective-permute-start | bytes 786440 | tf_op jit(solution)/shard_map/ppermute | solution.py:12
  (7 other events, 6.3 us)
Sparse Core Ops, SparseCore 0:
  132.7 110.1 reduce-scatter.1
where the time goes:
time: 307 us; the launch traced here: 302 us
  blocking collectives  124 us (40%)
  starting transfers between devices  51 us (17%)
  waiting for transfers between devices  43.9 us (14%)
  matrix products  26.5 us (9%)
  local copies, waits for them, and re-layouts  24.8 us (8%)
  other arithmetic  17.7 us (6%)
  between operations  14.4 us (5%)
    psum x1, blocking collectives, per_device(): lax.psum((router_term, gain_term), ('expert', 'dp'))  124 us
    ppermute x6, waiting for transfers between devices, partner_2(): return lax.ppermute(value, axis, pairs)  34.4 us
    ppermute x6, starting transfers between devices, partner_2(): return lax.ppermute(value, axis, pairs)  31.4 us
    dot_general x5, matrix products, matmul_right_t(): lax.dot_general(left, right, (((1,), (1,)), ((), ())), preferred_element_...  11 us
    dot_general x5, matrix products, matmul(): return jnp.dot(left, right, preferred_element_type=jnp.float32)  10.8 us
    all_to_all x1, starting transfers between devices, per_device(): lax.all_to_all(send, 'expert', split_axis=0, concat_axis=0, tiled=True)  6.65 us
    unnamed x57, local copies, waits for them, and re-layouts  6.14 us
  transfers between devices with their start and end apart: 11, of which 8 were waited for; matrix products, arithmetic and copies ran while one was open for 14% of the time, Pallas kernels for 0%

commit v1 on v0

v1 whole, which is shorter than its diff:
```python
import functools

import jax
import jax.numpy as jnp
from jax import lax
from jax.experimental import pallas as pl
from jax.experimental.pallas import tpu as pltpu
from jax.sharding import PartitionSpec as P

norm_eps = 1e-06
MESH = pl.DeviceIdType.MESH
BF = jnp.bfloat16
F32 = jnp.float32


def dot(left, right):
    return jnp.dot(left, right, preferred_element_type=F32)


def dot_rt(left, right):
    return lax.dot_general(left, right, (((1,), (1,)), ((), ())), preferred_element_type=F32)


def dot_lt(left, right):
    return lax.dot_general(left, right, (((0,), (0,)), ((), ())), preferred_element_type=F32)


def loop(count, body):
    for i in range(count):
        body(i)


class Copies:
    def __init__(self, send_sems, recv_sems):
        self.send_sems, self.recv_sems, self.used = send_sems, recv_sems, 0

    def make(self, src, dst, device):
        k = self.used
        self.used += 1
        return pltpu.make_async_remote_copy(
            src_ref=src,
            dst_ref=dst,
            send_sem=self.send_sems.at[k],
            recv_sem=self.recv_sems.at[k],
            device_id=device,
            device_id_type=MESH,
        )


N_SEM = 80


def kernel(
    hid, ids, cot, gain, rw, skip_h, gate_h, up_h, down_h,
    out_o, hg_o, sg_o, rg_o, gg_o,
    skip_v, gate_v, up_v, down_v,
    mir, hid_x, mir_x, jt,
    a0, a1, sl,
    gsend, grecv, nsend, nrecv, osend, orecv, bsend, brecv,
    ga, act, gg, gu,
    acc, normed, gn,
    rgs, rgx, rgr, rgy, rgf, rgo,
    gmh, gmx, gm2,
    mgs, mgr, own_g,
    pa, ra, pa2, ra2, pb, rb, pb2, rb2, fin, fin_x,
    local_sems, send_sems, recv_sems,
):
    T, D = hid.shape
    FF = gate_v.shape[1]
    E = 8
    CAP = nsend.shape[1]
    HALF = E // 2 * CAP
    W = D // 4
    H = D // 2
    n_sec = lax.axis_size("section")
    s = lax.axis_index("section")
    e = lax.axis_index("expert")
    d = lax.axis_index("dp")
    x, yh = e // 2, e % 2
    yl, c = d // 2, d % 2
    y = yh * 2 + yl
    upper = s >= n_sec // 2
    lower = s < n_sec // 2

    mirror_dev = (n_sec - 1 - s, e, d)
    core_dev = (s, e, d + 1 - 2 * c)

    def peer(dx, f):
        return (s, ((x + dx) % 4) * 2 + (yh + f) % 2, (d + 2 * f) % 4)

    def peer_y(dy):
        yy = (y + dy) % 4
        return (s, x * 2 + yy // 2, (yy % 2) * 2 + c)

    cp = Copies(send_sems, recv_sems)
    started = []

    def go(copy):
        copy.start()
        started.append(copy)

    loads = [
        pltpu.make_async_copy(src, dst, local_sems.at[i])
        for i, (src, dst) in enumerate(
            [(skip_h, skip_v), (down_h, down_v), (gate_h, gate_v), (up_h, up_v)]
        )
    ]
    for load in loads:
        load.start()

    barrier = pltpu.get_barrier_semaphore()
    greeted = [mirror_dev, core_dev]
    greeted += [peer(dx, f) for f in range(2) for dx in range(4) if (dx, f) != (0, 0)]
    greeted += [(s, e, (d + 2) % 4), (s, x * 2 + (yh + 1) % 2, d)]
    for device in greeted:
        pl.semaphore_signal(barrier, inc=1, device_id=device, device_id_type=MESH)
    pl.semaphore_wait(barrier, len(greeted))

    mirror_in = [cp.make(hid.at[:, pl.ds(j * W, W)], mir.at[j], mirror_dev) for j in range(4)]

    @pl.when(lower)
    def _():
        for copy in mirror_in:
            copy.start()

    hid_cp = cp.make(hid, hid_x, core_dev)
    go(hid_cp)

    def relative(names):
        dx = ((names >> 1) - x + 4) & 3
        f = ((names & 1) - yh + 2) & 1
        return f * 4 + dx

    id0, id1 = ids[:, 0:1], ids[:, 1:2]
    rel0, rel1 = relative(id0), relative(id1)
    lane = lax.broadcasted_iota(jnp.int32, (T, 128), 1)
    row = lax.broadcasted_iota(jnp.int32, (T, 128), 0)
    c0, c1 = rel0 == lane, rel1 == lane
    counts = jnp.where(c0, 1.0, 0.0) + jnp.where(c1, 1.0, 0.0)
    earlier = jnp.where(lane < row, 1.0, 0.0).astype(BF)
    before = dot(earlier, counts.astype(BF))
    rank0 = jnp.sum(jnp.where(c0, before, 0.0), axis=1, keepdims=True)
    rank1 = jnp.sum(jnp.where(c1, before, 0.0), axis=1, keepdims=True)
    slots = lax.broadcasted_iota(jnp.int32, (T, E * CAP), 1).astype(F32)
    at0 = jnp.where(rel0.astype(F32) * CAP + rank0 == slots, 1.0, 0.0)
    at1 = jnp.where(rel1.astype(F32) * CAP + rank1 == slots, 1.0, 0.0)
    a0[...] = at0.astype(BF)
    a1[...] = at1.astype(BF)
    eye = jnp.where(lane == row, 1.0, 0.0).astype(BF)
    sl[...] = dot_lt((at0 + at1).astype(BF), eye).astype(BF)

    order = [(2, 1), (2, 0), (1, 1), (3, 1), (1, 0), (3, 0), (0, 1)]

    def label(dx, f):
        return f * 4 + dx

    def place(rows, send, recv):
        def tile(i):
            cols = pl.ds(i * W, W)
            placed = dot(sl[...], rows[:, cols]).astype(BF)
            for o in range(E):
                block = placed[o * CAP : (o + 1) * CAP, :]
                if o == 0:
                    recv[0, :, cols] = block
                else:
                    send[o, :, cols] = block

        loop(D // W, tile)

    def dispatch(send, recv):
        copies = {}
        for dx, f in order:
            o = label(dx, f)
            copies[o] = cp.make(send.at[o], recv.at[o], peer(dx, f))
            go(copies[o])
        return copies

    def give_back(send, recv, copies, f):
        for dx, ff in order:
            if ff == f:
                o = label(dx, ff)
                copies[o] = cp.make(send.at[o], recv.at[o], peer((4 - dx) % 4, f))
                go(copies[o])

    place(cot, gsend, grecv)
    g_cp = dispatch(gsend, grecv)

    loads[0].wait()

    def own_mix(i):
        cols = pl.ds(i * W, W)
        acc[:, cols] = dot(hid[...], skip_v[0:D, cols])

    loop(D // W, own_mix)

    def turn(rows, at, col0):
        jt[pl.ds(at, rows.shape[1]), pl.ds(col0, T)] = rows.T

    loop(4, lambda j: turn(hid[:, j * W : (j + 1) * W], j * W, 0))
    hid_cp.wait_recv()
    loop(4, lambda j: turn(hid_x[:, j * W : (j + 1) * W], j * W, T))

    loads[1].wait()
    for o in g_cp:
        g_cp[o].wait_recv()

    def grad_act(i):
        cols = pl.ds(i * W, W)
        rows = grecv[...].reshape(E * CAP, D)
        ga[:, cols] = dot_rt(rows, down_v[cols, :])

    loop(FF // W, grad_act)

    mir_cp = cp.make(mir, mir_x, core_dev)

    @pl.when(upper)
    def _():
        for j in range(4):
            mirror_in[j].wait_recv()

            def add_mix(i, j=j):
                cols = pl.ds(i * W, W)
                acc[:, cols] += dot(mir[j], skip_v[D + j * W : D + (j + 1) * W, cols])

            loop(D // W, add_mix)
        mir_cp.start()

    wide = acc[...].astype(BF).astype(F32)
    acc[...] = wide
    inv_rms = lax.rsqrt(jnp.mean(wide * wide, axis=1, keepdims=True) + norm_eps)
    normed[...] = (wide * inv_rms * gain[...]).astype(BF)

    place(normed, nsend, nrecv)
    n_cp = dispatch(nsend, nrecv)

    lane8 = lax.broadcasted_iota(jnp.int32, (T, 8), 1)
    k0, k1 = id0 == lane8, id1 == lane8
    logits = dot(normed[...], rw[...])
    s0 = jax.nn.sigmoid(jnp.sum(jnp.where(k0, logits, 0.0), axis=1, keepdims=True))
    s1 = jax.nn.sigmoid(jnp.sum(jnp.where(k1, logits, 0.0), axis=1, keepdims=True))
    total = s0 + s1
    w0, w1 = s0 / total, s1 / total

    @pl.when(upper)
    def _():
        loop(4, lambda j: turn(mir[j], D + j * W, 0))

    @pl.when(lower)
    def _():
        jt[D : 2 * D, :] = jnp.zeros((D, 2 * T), BF)

    loads[2].wait()
    loads[3].wait()

    o_cp, b_cp = {}, {}
    for f in range(2):
        blocks = slice(f * 4, f * 4 + 4)
        rows = slice(f * HALF, (f + 1) * HALF)
        for o in range(f * 4, f * 4 + 4):
            if o != 0:
                n_cp[o].wait_recv()

        def hidden_units(i):
            cols = pl.ds(i * W, W)
            frames = nrecv[blocks].reshape(HALF, D)
            pre_gate = dot(frames, gate_v[:, cols])
            pre_up = dot(frames, up_v[:, cols])
            grad = ga[rows, cols]
            sig = jax.nn.sigmoid(pre_gate)
            silu = pre_gate * sig
            act[rows, cols] = (silu * pre_up).astype(BF)
            gg[rows, cols] = (grad * pre_up * sig * (1.0 + pre_gate * (1.0 - sig))).astype(BF)
            gu[rows, cols] = (grad * silu).astype(BF)

        loop(FF // W, hidden_units)

        def split(values, send, recv, cols):
            for k in range(4):
                block = values[k * CAP : (k + 1) * CAP, :]
                if f == 0 and k == 0:
                    recv[0, :, cols] = block
                else:
                    send[f * 4 + k, :, cols] = block

        def outputs(i):
            cols = pl.ds(i * W, W)
            split(dot(act[rows, :], down_v[:, cols]).astype(BF), osend, orecv, cols)

        loop(D // W, outputs)
        give_back(osend, orecv, o_cp, f)

        def inputs(i):
            cols = pl.ds(i * W, W)
            grads = dot_rt(gg[rows, :], gate_v[cols, :]) + dot_rt(gu[rows, :], up_v[cols, :])
            split(grads.astype(BF), bsend, brecv, cols)

        loop(D // W, inputs)
        give_back(bsend, brecv, b_cp, f)

    @pl.when(upper)
    def _():
        mir_cp.wait_recv()
        loop(4, lambda j: turn(mir_x[j], D + j * W, T))

    for o in o_cp:
        o_cp[o].wait_recv()
    grad_w0, grad_w1 = 0.0, 0.0
    for i in range(D // W):
        cols = slice(i * W, (i + 1) * W)
        rows_o = orecv[:, :, cols].reshape(E * CAP, W)
        p0, p1 = dot(a0[...], rows_o), dot(a1[...], rows_o)
        out_o[:, cols] = (acc[:, cols] + w0 * p0 + w1 * p1).astype(BF)
        grad_out = cot[:, cols].astype(F32)
        grad_w0 += jnp.sum(grad_out * p0, axis=1, keepdims=True)
        grad_w1 += jnp.sum(grad_out * p1, axis=1, keepdims=True)
    weighted = w0 * grad_w0 + w1 * grad_w1
    gl0 = (grad_w0 - weighted) / total * s0 * (1.0 - s0)
    gl1 = (grad_w1 - weighted) / total * s1 * (1.0 - s1)
    grad_logits = (jnp.where(k0, gl0, 0.0) + jnp.where(k1, gl1, 0.0)).astype(BF)

    for o in b_cp:
        b_cp[o].wait_recv()
    mean_term = 0.0
    for i in range(D // W):
        cols = slice(i * W, (i + 1) * W)
        rows_b = brecv[:, :, cols].reshape(E * CAP, W)
        grad_normed = w0 * dot(a0[...], rows_b) + w1 * dot(a1[...], rows_b)
        grad_normed += dot_rt(grad_logits, rw[cols, :])
        unit = acc[:, cols] * inv_rms
        gain_term = jnp.sum(grad_normed * unit, axis=0, keepdims=True)
        router_term = dot_lt(grad_logits, normed[:, cols])
        both = jnp.concatenate([router_term, jnp.broadcast_to(gain_term, (8, W))], axis=0)
        rgs[i // 2, :, (i % 2) * W : (i % 2 + 1) * W] = both.astype(BF)
        grad_unit = grad_normed * gain[:, cols]
        gn[:, cols] = grad_unit
        mean_term += jnp.sum(grad_unit * unit, axis=1, keepdims=True)
    mean_term = mean_term / D
    rg_core = cp.make(rgs.at[1 - c], rgx, core_dev)
    go(rg_core)
    for i in range(D // W):
        cols = slice(i * W, (i + 1) * W)
        unit = acc[:, cols] * inv_rms
        grad_mixed = cot[:, cols].astype(F32) + inv_rms * (gn[:, cols] - unit * mean_term)
        gmh[i // 2, :, (i % 2) * W : (i % 2 + 1) * W] = grad_mixed.astype(BF)
    gm_core = cp.make(gmh.at[1 - c], gmx, core_dev)
    go(gm_core)

    grad_mixed = jnp.concatenate([gmh[0], gmh[1]], axis=1)

    mirror_out = [cp.make(mgs.at[j], mgr.at[j], mirror_dev) for j in range(4)]

    @pl.when(upper)
    def _():
        for j in range(4):
            mgs[j] = dot_rt(grad_mixed, skip_v[D + j * W : D + (j + 1) * W, :]).astype(BF)
            mirror_out[j].start()

    rg_core.wait_recv()
    rgr[x] = (rgs[c].astype(F32) + rgx[...].astype(F32)).astype(BF)
    rg_x = [cp.make(rgr.at[x], rgr.at[x], peer(dx, 0)) for dx in (2, 1, 3)]
    for copy in rg_x:
        go(copy)

    gm_core.wait_recv()
    gm2[0:T, :] = gmh[c]
    gm2[T : 2 * T, :] = gmx[...]
    a1_cp, b1_cp = {}, {}
    for dx in (2, 1, 3, 0):
        xx = (x + dx) % 4
        part = dot(jt[pl.ds(pl.multiple_of(xx * 4 * T, 4 * T), 4 * T), :], gm2[...])
        pa[dx] = part[:, :W].astype(BF)
        for yy in range(4):
            pb[yy, dx] = part[yy * T : (yy + 1) * T, W:].astype(BF)
        if dx != 0:
            a1_cp[dx] = cp.make(pa.at[dx], ra.at[dx], peer(dx, 0))
            go(a1_cp[dx])
    for dy in (2, 1, 3):
        b1_cp[dy] = cp.make(pb.at[(y + dy) % 4], rb.at[dy], peer_y(dy))
        go(b1_cp[dy])

    def own_grad(j):
        cols = pl.ds(j * W, W)
        own_g[:, cols] = dot_rt(grad_mixed, skip_v[cols, :]).astype(BF)

    loop(4, own_grad)

    for copy in rg_x:
        copy.wait_recv()
    sum_x = rgr[0].astype(F32) + rgr[1].astype(F32) + rgr[2].astype(F32) + rgr[3].astype(F32)
    rgy[y] = sum_x.astype(BF)
    rg_y = [cp.make(rgy.at[y], rgy.at[y], peer_y(dy)) for dy in (2, 1, 3)]
    for copy in rg_y:
        go(copy)

    for dx in (1, 3, 2):
        a1_cp[dx].wait_recv()
    sum_a = pa[0].astype(F32) + ra[1].astype(F32) + ra[2].astype(F32) + ra[3].astype(F32)
    for yy in range(4):
        pa2[yy] = sum_a[yy * T : (yy + 1) * T, :].astype(BF)
    a2_cp = {}
    for dy in (2, 1, 3):
        a2_cp[dy] = cp.make(pa2.at[(y + dy) % 4], ra2.at[dy], peer_y(dy))
        go(a2_cp[dy])
    for dy in (1, 3, 2):
        b1_cp[dy].wait_recv()
    b2_cp = {}
    for dx in (2, 1, 3, 0):
        sum_b = pb[y, dx].astype(F32)
        for dy in (1, 2, 3):
            sum_b += rb[dy, dx].astype(F32)
        pb2[dx] = sum_b.astype(BF)
        if dx != 0:
            b2_cp[dx] = cp.make(pb2.at[dx], rb2.at[dx], peer(dx, 0))
            go(b2_cp[dx])

    for copy in rg_y:
        copy.wait_recv()
    rgf[...] = rgy[0].astype(F32) + rgy[1].astype(F32) + rgy[2].astype(F32) + rgy[3].astype(F32)
    rg_out = cp.make(rgf, rgo, core_dev)
    go(rg_out)

    for dy in (1, 3, 2):
        a2_cp[dy].wait_recv()
    res_a = pa2[y].astype(F32)
    for dy in (1, 2, 3):
        res_a += ra2[dy].astype(F32)
    for dx in (1, 3, 2):
        b2_cp[dx].wait_recv()
    res_b = pb2[0].astype(F32)
    for dx in (1, 2, 3):
        res_b += rb2[dx].astype(F32)
    for h in range(2):
        fin[h, :, 0:W] = res_a[h * (T // 2) : (h + 1) * (T // 2), :]
        fin[h, :, W:H] = res_b[h * (T // 2) : (h + 1) * (T // 2), :]
    fin_cp = cp.make(fin.at[1 - c], fin_x, core_dev)
    go(fin_cp)

    @pl.when(upper)
    def _():
        hg_o[...] = own_g[...]

    @pl.when(lower)
    def _():
        for j in range(4):
            mirror_out[j].wait_recv()
            cols = slice(j * W, (j + 1) * W)
            hg_o[:, cols] = (own_g[:, cols].astype(F32) + mgr[j].astype(F32)).astype(BF)

    here = pl.ds(pl.multiple_of(c * H, H), H)
    there = pl.ds(pl.multiple_of((1 - c) * H, H), H)
    rg_out.wait_recv()
    rg_o[:, here] = rgf[0:8, :]
    rg_o[:, there] = rgo[0:8, :]
    gg_o[:, here] = rgf[8:9, :]
    gg_o[:, there] = rgo[8:9, :]
    fin_cp.wait_recv()
    sg_o[:, here] = fin[c]
    sg_o[:, there] = fin_x[...]

    for copy in started:
        copy.wait_send()

    @pl.when(lower)
    def _():
        for copy in mirror_in:
            copy.wait_send()

    @pl.when(upper)
    def _():
        mir_cp.wait_send()
        for copy in mirror_out:
            copy.wait_send()


def per_device(
    hidden, expert_ids, cotangent, skip_weight, norm_gain, router_weight,
    gate_weight, up_weight, down_weight,
):
    T, D = hidden.shape[1:]
    FF = gate_weight.shape[-1]
    E = lax.axis_size("expert")
    CAP = min(T, 3 * T // E)
    W, H = D // 4, D // 2
    slots = E * CAP
    vmem = pl.BlockSpec(memory_space=pltpu.VMEM)
    anywhere = pl.BlockSpec(memory_space=pl.ANY)
    a2a = pltpu.VMEM((E, CAP, D), BF)
    scratch = [
        pltpu.VMEM((2 * D, D), BF), pltpu.VMEM((D, FF), BF), pltpu.VMEM((D, FF), BF), pltpu.VMEM((FF, D), BF),
        pltpu.VMEM((4, T, W), BF), pltpu.VMEM((T, D), BF), pltpu.VMEM((4, T, W), BF), pltpu.VMEM((2 * D, 2 * T), BF),
        pltpu.VMEM((T, slots), BF), pltpu.VMEM((T, slots), BF), pltpu.VMEM((slots, T), BF),
        a2a, a2a, a2a, a2a, a2a, a2a, a2a, a2a,
        pltpu.VMEM((slots, FF), F32), pltpu.VMEM((slots, FF), BF), pltpu.VMEM((slots, FF), BF), pltpu.VMEM((slots, FF), BF),
        pltpu.VMEM((T, D), F32), pltpu.VMEM((T, D), BF), pltpu.VMEM((T, D), F32),
        pltpu.VMEM((2, 16, H), BF), pltpu.VMEM((16, H), BF), pltpu.VMEM((4, 16, H), BF), pltpu.VMEM((4, 16, H), BF),
        pltpu.VMEM((16, H), F32), pltpu.VMEM((16, H), F32),
        pltpu.VMEM((2, T, H), BF), pltpu.VMEM((T, H), BF), pltpu.VMEM((2 * T, H), BF),
        pltpu.VMEM((4, T, W), BF), pltpu.VMEM((4, T, W), BF), pltpu.VMEM((T, D), BF),
        pltpu.VMEM((4, 4 * T, W), BF), pltpu.VMEM((4, 4 * T, W), BF), pltpu.VMEM((4, T, W), BF), pltpu.VMEM((4, T, W), BF),
        pltpu.VMEM((4, 4, T, W), BF), pltpu.VMEM((4, 4, T, W), BF), pltpu.VMEM((4, T, W), BF), pltpu.VMEM((4, T, W), BF),
        pltpu.VMEM((2, T // 2, H), F32), pltpu.VMEM((T // 2, H), F32),
        pltpu.SemaphoreType.DMA((4,)), pltpu.SemaphoreType.DMA((N_SEM,)), pltpu.SemaphoreType.DMA((N_SEM,)),
    ]
    out, hidden_grad, skip_grad, router, gain = pl.pallas_call(
        kernel,
        out_shape=(
            jax.ShapeDtypeStruct((T, D), BF),
            jax.ShapeDtypeStruct((T, D), BF),
            jax.ShapeDtypeStruct((T // 2, D), F32),
            jax.ShapeDtypeStruct((8, D), F32),
            jax.ShapeDtypeStruct((1, D), F32),
        ),
        in_specs=[vmem] * 5 + [anywhere] * 4,
        out_specs=[vmem] * 5,
        scratch_shapes=scratch,
        compiler_params=pltpu.CompilerParams(
            collective_id=0, has_side_effects=True, vmem_limit_bytes=60 * 1024 * 1024
        ),
    )(
        hidden[0], expert_ids[0], cotangent[0], norm_gain, router_weight[0],
        skip_weight[0], gate_weight[0, 0], up_weight[0, 0], down_weight[0, 0],
    )
    return (out[None], hidden_grad[None], skip_grad[None], router.T[None], gain)


def solution(mesh):
    return jax.shard_map(
        per_device,
        mesh=mesh,
        in_specs=(
            P("section", ("expert", "dp"), None),
            P("section", ("expert", "dp"), None),
            P("section", ("expert", "dp"), None),
            P("section", None, None),
            P("section", None),
            P("section", None, None),
            P("section", "expert", None, None),
            P("section", "expert", None, None),
            P("section", "expert", None, None),
        ),
        out_specs=(
            P("section", ("expert", "dp"), None),
            P("section", ("expert", "dp"), None),
            P("section", ("expert", "dp"), None),
            P("section", None, None),
            P("section", None),
        ),
        check_vma=False,
    )
```

time: 307 us -> 95.6 us (0.31); the launches traced: 302 us -> 95.2 us
  blocking collectives: 124 us -> 0 us
  Pallas kernels: 0 us -> 84 us
  starting transfers between devices: 51 us -> 0 us
  waiting for transfers between devices: 43.9 us -> 0 us
  matrix products: 26.5 us -> 0 us
  other arithmetic: 17.7 us -> 0 us
  local copies, waits for them, and re-layouts: 24.8 us -> 10.6 us
  between operations: 14.4 us -> 0.64 us
    psum x1 -> x0, blocking collectives: 124 us -> none  [per_device(): lax.psum((router_term, gain_term), ('expert', 'dp'))]
    pallas_call x0 -> x1, Pallas kernels: none -> 84 us  [per_device(): pl.pallas_call(kernel, out_shape=(jax.ShapeDtypeStruct((T, D), BF), jax.S...]
    ppermute x6 -> x0, waiting for transfers between devices: 34.4 us -> none  [partner_2(): return lax.ppermute(value, axis, pairs)]
    ppermute x6 -> x0, starting transfers between devices: 31.4 us -> none  [partner_2(): return lax.ppermute(value, axis, pairs)]
    dot_general x12 -> x0, matrix products: 26.5 us -> none  [the longest x5 11 us: matmul_right_t(): lax.dot_general(left, right, (((1,), (1,)), ((), ())), preferred_element_...]
    all_to_all x4 -> x0, starting transfers between devices: 19.5 us -> none  [the longest x1 6.65 us: per_device(): lax.all_to_all(send, 'expert', split_axis=0, concat_axis=0, tiled=True)]
    reduce_sum x7 -> x0, other arithmetic: 9.46 us -> none  [the longest x1 4.01 us: section_back(): grad_weight = jnp.sum(grad_out[:, None, :] * picked_wide, axis=2)]
    all_to_all x4 -> x0, waiting for transfers between devices: 9.45 us -> none  [the longest x1 5.52 us: per_device(): lax.all_to_all(send, 'expert', split_axis=0, concat_axis=0, tiled=True)]
  transfers between devices with their start and end apart: 11 -> 0, of which waited for: 8 -> 0; matrix products, arithmetic and copies ran while one was open for 14% -> 0% of each run, Pallas kernels for 0% -> 0%
where the time goes in v1:
time: 95.6 us; the launch traced here: 95.2 us
  Pallas kernels  84 us (88%)
  local copies, waits for them, and re-layouts  10.6 us (11%)
    pallas_call x1, Pallas kernels, per_device(): pl.pallas_call(kernel, out_shape=(jax.ShapeDtypeStruct((T, D), BF), jax.S...  84 us
    unnamed x7, local copies, waits for them, and re-layouts  10.6 us

profile of v1, /device:TPU:1, one launch (start us, length us, event | category | flops | bytes accessed | tf_op | source)
XLA Modules:
  0.0 95.2 jit_solution(12860152006021055319)
XLA Ops:
  0.6 1.4 %copy.14 = s32[1,128,2]{2,1,0:T(8,128)} copy(s32[1,128,2]{1,2,0:T(2,128)} %param.10) | data formatting | bytes 2048 | tf_op args[1]
  2.0 1.6 %copy.15 = bf16[1,1024,8]{2,1,0:T(8,128)(2,1)} copy(bf16[1,1024,8]{1,2,0:T(8,128)(2,1)} %param.14) | data formatting | bytes 32768 | tf_op args[5]
  3.6 84.0 %shard_map.128 = (bf16[128,1024]{1,0:T(8,128)(2,1)}, bf16[128,1024]{1,0:T(8,128)(2,1)}, f32[64,1024]{1,0:T(8,128)}, f32[8,1024]{1,0:T(8,128)}, f32[1,1024]{1,0:T(1,128)}) custom-call(bf16[128,1024]{1,0:T(8,128)(2,1)} %bitcast.20, s32[128,2]{1,0:T(8,128)} %bitcast.19, bf16[128,1024]{1,0:T(8,128)(2,1)} %bitcast.21, f32[1,1024]{1,0:T(1,128)} %gain.1, ...), custom_call_target="tpu_custom_call" | custom-call | tf_op jit(solution)/shard_map/pallas_call | solution.py:504
  87.6 1.7 %copy.21 = bf16[1,128,1024]{2,1,0:T(8,128)(2,1)} copy(bf16[1,128,1024]{2,1,0:T(8,128)(2,1)} %bitcast.24) | data formatting | bytes 524288
  89.2 1.7 %copy.22 = bf16[1,128,1024]{2,1,0:T(8,128)(2,1)} copy(bf16[1,128,1024]{2,1,0:T(8,128)(2,1)} %bitcast.23) | data formatting | bytes 524288
  90.9 1.7 %copy.23 = f32[1,64,1024]{2,1,0:T(8,128)} copy(f32[1,64,1024]{2,1,0:T(8,128)} %bitcast.22) | data formatting | bytes 524288
  92.6 1.4 %copy.24 = f32[1,1024,8]{1,2,0:T(8,128)} copy(f32[1,1024,8]{1,2,0:T(8,128)} %bitcast.25) | data formatting | bytes 65536
  94.0 1.3 %copy.25 = f32[1,1024]{1,0:T(1,128)} copy(f32[1,1024]{1,0:T(1,128)} %get-tuple-element.24) | data formatting | bytes 8192

commit v2 on v1

--- a/solution.py
+++ b/solution.py
@@ -56,7 +56,7 @@
     skip_v, gate_v, up_v, down_v,
     mir, hid_x, mir_x, jt,
     a0, a1, sl,
-    gsend, grecv, nsend, nrecv, osend, orecv, bsend, brecv,
+    gsend, grecv, nsend, nrecv, osend, orecv, bsend, brecv, wsend, wrecv,
     ga, act, gg, gu,
     acc, normed, gn,
     rgs, rgx, rgr, rgy, rgf, rgo,
@@ -131,10 +131,12 @@
         f = ((names & 1) - yh + 2) & 1
         return f * 4 + dx
 
-    id0, id1 = ids[:, 0:1], ids[:, 1:2]
-    rel0, rel1 = relative(id0), relative(id1)
     lane = lax.broadcasted_iota(jnp.int32, (T, 128), 1)
     row = lax.broadcasted_iota(jnp.int32, (T, 128), 0)
+    eye = jnp.where(lane == row, 1.0, 0.0).astype(BF)
+    names = dot_rt(eye, ids[...].astype(F32).astype(BF)).astype(jnp.int32)
+    id0, id1 = names[:, 0:1], names[:, 1:2]
+    rel0, rel1 = relative(id0), relative(id1)
     c0, c1 = rel0 == lane, rel1 == lane
     counts = jnp.where(c0, 1.0, 0.0) + jnp.where(c1, 1.0, 0.0)
     earlier = jnp.where(lane < row, 1.0, 0.0).astype(BF)
@@ -146,10 +148,9 @@
     at1 = jnp.where(rel1.astype(F32) * CAP + rank1 == slots, 1.0, 0.0)
     a0[...] = at0.astype(BF)
     a1[...] = at1.astype(BF)
-    eye = jnp.where(lane == row, 1.0, 0.0).astype(BF)
     sl[...] = dot_lt((at0 + at1).astype(BF), eye).astype(BF)
 
-    order = [(2, 1), (2, 0), (1, 1), (3, 1), (1, 0), (3, 0), (0, 1)]
+    order = [(2, 0), (1, 0), (3, 0), (2, 1), (1, 1), (3, 1), (0, 1)]
 
     def label(dx, f):
         return f * 4 + dx
@@ -235,7 +236,7 @@
 
     lane8 = lax.broadcasted_iota(jnp.int32, (T, 8), 1)
     k0, k1 = id0 == lane8, id1 == lane8
-    logits = dot(normed[...], rw[...])
+    logits = dot_rt(normed[...], rw[...])
     s0 = jax.nn.sigmoid(jnp.sum(jnp.where(k0, logits, 0.0), axis=1, keepdims=True))
     s1 = jax.nn.sigmoid(jnp.sum(jnp.where(k1, logits, 0.0), axis=1, keepdims=True))
     total = s0 + s1
@@ -251,6 +252,14 @@
 
     loads[2].wait()
     loads[3].wait()
+
+    def split(values, send, recv, cols, f):
+        for k in range(4):
+            block = values[k * CAP : (k + 1) * CAP, :]
+            if f == 0 and k == 0:
+                recv[0, :, cols] = block
+            else:
+                send[f * 4 + k, :, cols] = block
 
     o_cp, b_cp = {}, {}
     for f in range(2):
@@ -274,45 +283,46 @@
 
         loop(FF // W, hidden_units)
 
-        def split(values, send, recv, cols):
-            for k in range(4):
-                block = values[k * CAP : (k + 1) * CAP, :]
-                if f == 0 and k == 0:
-                    recv[0, :, cols] = block
-                else:
-                    send[f * 4 + k, :, cols] = block
-
-        def outputs(i):
-            cols = pl.ds(i * W, W)
-            split(dot(act[rows, :], down_v[:, cols]).astype(BF), osend, orecv, cols)
-
-        loop(D // W, outputs)
-        give_back(osend, orecv, o_cp, f)
-
         def inputs(i):
             cols = pl.ds(i * W, W)
             grads = dot_rt(gg[rows, :], gate_v[cols, :]) + dot_rt(gu[rows, :], up_v[cols, :])
-            split(grads.astype(BF), bsend, brecv, cols)
+            split(grads.astype(BF), bsend, brecv, cols, f)
 
         loop(D // W, inputs)
         give_back(bsend, brecv, b_cp, f)
 
+    w_cp = {}
+    for f in range(2):
+        blocks = slice(f * 4, f * 4 + 4)
+        rows = slice(f * HALF, (f + 1) * HALF)
+        along = 0.0
+        for i in range(D // W):
+            cols = slice(i * W, (i + 1) * W)
+            values = dot(act[rows, :], down_v[:, cols]).astype(BF)
+            split(values, osend, orecv, cols, f)
+            grads = grecv[blocks, :, cols].reshape(HALF, W).astype(F32)
+            along += jnp.sum(values.astype(F32) * grads, axis=1, keepdims=True)
+        high = along.astype(BF)
+        low = (along - high.astype(F32)).astype(BF)
+        half = lax.broadcasted_iota(jnp.int32, (HALF, 128), 1) < 64
+        split(jnp.where(half, high, low), wsend, wrecv, slice(0, 128), f)
+        give_back(wsend, wrecv, w_cp, f)
+    for o in b_cp:
+        b_cp[o].wait_send()
+    for f in range(2):
+        give_back(osend, orecv, o_cp, f)
+
     @pl.when(upper)
     def _():
         mir_cp.wait_recv()
         loop(4, lambda j: turn(mir_x[j], D + j * W, T))
 
-    for o in o_cp:
-        o_cp[o].wait_recv()
-    grad_w0, grad_w1 = 0.0, 0.0
-    for i in range(D // W):
-        cols = slice(i * W, (i + 1) * W)
-        rows_o = orecv[:, :, cols].reshape(E * CAP, W)
-        p0, p1 = dot(a0[...], rows_o), dot(a1[...], rows_o)
-        out_o[:, cols] = (acc[:, cols] + w0 * p0 + w1 * p1).astype(BF)
-        grad_out = cot[:, cols].astype(F32)
-        grad_w0 += jnp.sum(grad_out * p0, axis=1, keepdims=True)
-        grad_w1 += jnp.sum(grad_out * p1, axis=1, keepdims=True)
+    for o in w_cp:
+        w_cp[o].wait_recv()
+    rows_w = wrecv[...].reshape(E * CAP, 128)
+    t0, t1 = dot(a0[...], rows_w), dot(a1[...], rows_w)
+    grad_w0 = t0[:, 0:1] + t0[:, 64:65]
+    grad_w1 = t1[:, 0:1] + t1[:, 64:65]
     weighted = w0 * grad_w0 + w1 * grad_w1
     gl0 = (grad_w0 - weighted) / total * s0 * (1.0 - s0)
     gl1 = (grad_w1 - weighted) / total * s1 * (1.0 - s1)
@@ -325,7 +335,7 @@
         cols = slice(i * W, (i + 1) * W)
         rows_b = brecv[:, :, cols].reshape(E * CAP, W)
         grad_normed = w0 * dot(a0[...], rows_b) + w1 * dot(a1[...], rows_b)
-        grad_normed += dot_rt(grad_logits, rw[cols, :])
+        grad_normed += dot(grad_logits, rw[:, cols])
         unit = acc[:, cols] * inv_rms
         gain_term = jnp.sum(grad_normed * unit, axis=0, keepdims=True)
         router_term = dot_lt(grad_logits, normed[:, cols])
@@ -383,6 +393,14 @@
         own_g[:, cols] = dot_rt(grad_mixed, skip_v[cols, :]).astype(BF)
 
     loop(4, own_grad)
+
+    for o in o_cp:
+        o_cp[o].wait_recv()
+    for i in range(D // W):
+        cols = slice(i * W, (i + 1) * W)
+        rows_o = orecv[:, :, cols].reshape(E * CAP, W)
+        p0, p1 = dot(a0[...], rows_o), dot(a1[...], rows_o)
+        out_o[:, cols] = (acc[:, cols] + w0 * p0 + w1 * p1).astype(BF)
 
     for copy in rg_x:
         copy.wait_recv()
@@ -458,7 +476,8 @@
     sg_o[:, there] = fin_x[...]
 
     for copy in started:
-        copy.wait_send()
+        if not any(copy is b_cp[o] for o in b_cp):
+            copy.wait_send()
 
     @pl.when(lower)
     def _():
@@ -470,6 +489,11 @@
         mir_cp.wait_send()
         for copy in mirror_out:
             copy.wait_send()
+
+
+def hand_on(*refs):
+    for source, target in zip(refs[:5], refs[5:]):
+        target[...] = source[...]
 
 
 def per_device(
@@ -489,7 +513,7 @@
         pltpu.VMEM((2 * D, D), BF), pltpu.VMEM((D, FF), BF), pltpu.VMEM((D, FF), BF), pltpu.VMEM((FF, D), BF),
         pltpu.VMEM((4, T, W), BF), pltpu.VMEM((T, D), BF), pltpu.VMEM((4, T, W), BF), pltpu.VMEM((2 * D, 2 * T), BF),
         pltpu.VMEM((T, slots), BF), pltpu.VMEM((T, slots), BF), pltpu.VMEM((slots, T), BF),
-        a2a, a2a, a2a, a2a, a2a, a2a, a2a, a2a,
+        a2a, a2a, a2a, a2a, a2a, a2a, a2a, a2a, pltpu.VMEM((E, CAP, 128), BF), pltpu.VMEM((E, CAP, 128), BF),
         pltpu.VMEM((slots, FF), F32), pltpu.VMEM((slots, FF), BF), pltpu.VMEM((slots, FF), BF), pltpu.VMEM((slots, FF), BF),
         pltpu.VMEM((T, D), F32), pltpu.VMEM((T, D), BF), pltpu.VMEM((T, D), F32),
         pltpu.VMEM((2, 16, H), BF), pltpu.VMEM((16, H), BF), pltpu.VMEM((4, 16, H), BF), pltpu.VMEM((4, 16, H), BF),
@@ -501,7 +525,7 @@
         pltpu.VMEM((2, T // 2, H), F32), pltpu.VMEM((T // 2, H), F32),
         pltpu.SemaphoreType.DMA((4,)), pltpu.SemaphoreType.DMA((N_SEM,)), pltpu.SemaphoreType.DMA((N_SEM,)),
     ]
-    out, hidden_grad, skip_grad, router, gain = pl.pallas_call(
+    results = pl.pallas_call(
         kernel,
         out_shape=(
             jax.ShapeDtypeStruct((T, D), BF),
@@ -517,9 +541,15 @@
             collective_id=0, has_side_effects=True, vmem_limit_bytes=60 * 1024 * 1024
         ),
     )(
-        hidden[0], expert_ids[0], cotangent[0], norm_gain, router_weight[0],
+        hidden[0], expert_ids[0].T, cotangent[0], norm_gain, router_weight[0].T,
         skip_weight[0], gate_weight[0, 0], up_weight[0, 0], down_weight[0, 0],
     )
+    out, hidden_grad, skip_grad, router, gain = pl.pallas_call(
+        hand_on,
+        out_shape=tuple(jax.ShapeDtypeStruct(r.shape, r.dtype) for r in results),
+        in_specs=[vmem] * 5,
+        out_specs=[vmem] * 5,
+    )(*results)
     return (out[None], hidden_grad[None], skip_grad[None], router.T[None], gain)
 
 

time: 95.6 us -> 83.9 us (0.88)
  local copies, waits for them, and re-layouts: 10.6 us -> 0 us
    unnamed x7 -> x0, local copies, waits for them, and re-layouts: 10.6 us -> none
    pallas_call x1, Pallas kernels: 84 us -> 81.1 us  [per_device(): pl.pallas_call(kernel, out_shape=(jax.ShapeDtypeStruct((T, D), BF), jax.S...]
    pallas_call x0 -> x1, Pallas kernels: none -> 2.04 us  [per_device(): pl.pallas_call(hand_on, out_shape=tuple((jax.ShapeDtypeStruct(r.shape, r....]
where the time goes in v2:
time: 83.9 us; the launch traced here: 83.7 us
  Pallas kernels  83.1 us (99%)
    pallas_call x1, Pallas kernels, per_device(): pl.pallas_call(kernel, out_shape=(jax.ShapeDtypeStruct((T, D), BF), jax.S...  81.1 us
    pallas_call x1, Pallas kernels, per_device(): pl.pallas_call(hand_on, out_shape=tuple((jax.ShapeDtypeStruct(r.shape, r....  2.04 us

profile of v2, /device:TPU:1, one launch (start us, length us, event | category | flops | bytes accessed | tf_op | source)
XLA Modules:
  0.0 83.7 jit_solution(1210326745503903424)
XLA Ops:
  0.6 81.1 %shard_map.128 = (bf16[128,1024]{1,0:T(8,128)(2,1)}, bf16[128,1024]{1,0:T(8,128)(2,1)}, f32[64,1024]{1,0:T(8,128)}, f32[8,1024]{1,0:T(8,128)}, f32[1,1024]{1,0:T(1,128)}) custom-call(bf16[128,1024]{1,0:T(8,128)(2,1)} %bitcast.22, s32[2,128]{1,0:T(2,128)} %bitcast.25, bf16[128,1024]{1,0:T(8,128)(2,1)} %bitcast.23, f32[1,1024]{1,0:T(1,128)} %gain.1, ...), custom_call_target="tpu_custom_call" | custom-call | tf_op jit(solution)/shard_map/pallas_call | solution.py:528
  81.7 2.0 %shard_map.129 = (bf16[128,1024]{1,0:T(8,128)(2,1)}, bf16[128,1024]{1,0:T(8,128)(2,1)}, f32[64,1024]{1,0:T(8,128)}, f32[8,1024]{1,0:T(8,128)}, f32[1,1024]{1,0:T(1,128)}) custom-call(bf16[128,1024]{1,0:T(8,128)(2,1)} %get-tuple-element.15.refs_0_, bf16[128,1024]{1,0:T(8,128)(2,1)} %get-tuple-element.16.refs_1_, f32[64,1024]{1,0:T(8,128)} %get-tuple-element.17.refs_2_, ...), custom_call_target="tpu_custom_call" | custom-call | tf_op jit(solution)/shard_map/pallas_call | solution.py:547

commit v3 on v2

v3 whole, which is shorter than its diff:
```python
import functools

import jax
import jax.numpy as jnp
from jax import lax
from jax.experimental import pallas as pl
from jax.experimental.pallas import tpu as pltpu
from jax.sharding import PartitionSpec as P

norm_eps = 1e-06
MESH = pl.DeviceIdType.MESH
BF = jnp.bfloat16
F32 = jnp.float32


def dot(left, right):
    return jnp.dot(left, right, preferred_element_type=F32)


def dot_rt(left, right):
    return lax.dot_general(left, right, (((1,), (1,)), ((), ())), preferred_element_type=F32)


def dot_lt(left, right):
    return lax.dot_general(left, right, (((0,), (0,)), ((), ())), preferred_element_type=F32)


def loop(count, body):
    for i in range(count):
        body(i)


class Copies:
    def __init__(self, send_sems, recv_sems):
        self.send_sems, self.recv_sems, self.used = send_sems, recv_sems, 0

    def make(self, src, dst, device):
        k = self.used
        self.used += 1
        return pltpu.make_async_remote_copy(
            src_ref=src,
            dst_ref=dst,
            send_sem=self.send_sems.at[k],
            recv_sem=self.recv_sems.at[k],
            device_id=device,
            device_id_type=MESH,
        )


N_SEM = 104
DISTANCES = [(0, 0), (1, 0), (3, 0), (0, 1), (2, 1), (2, 0), (1, 1), (3, 1)]
GROUPS = [(0, 5), (5, 8)]
SEND_FIRST, SEND_LAST = [4, 3, 1, 2], [6, 7, 5]
O_FIRST, O_LAST = [3, 1, 2], [4, 6, 7, 5]


def kernel(
    hid, ids, cot, gain, rw, skip_h, gate_h, up_h, down_h,
    out_o, hg_o, sg_o, rg_o, gg_o,
    skip_v, gate_v, up_v, down_v,
    mir, jto, ja, jb,
    a0, a1, sl,
    gsend, grecv, nsend, nrecv, osend, orecv, bsend, brecv, wsend, wrecv,
    ga, act, gg, gu,
    acc, normed, gn,
    rgs, r1, r2,
    gmq, ga_x, gb_x,
    mgs, mgr, own_g,
    pa, pb, ra, rb,
    local_sems, send_sems, recv_sems,
):
    T, D = hid.shape
    FF = gate_v.shape[1]
    E = 8
    CAP = nsend.shape[1]
    HALF = E // 2 * CAP
    W = D // 4
    H = D // 2
    n_sec = lax.axis_size("section")
    s = lax.axis_index("section")
    e = lax.axis_index("expert")
    d = lax.axis_index("dp")
    x, yh = e // 2, e % 2
    yl, c = d // 2, d % 2
    y = yh * 2 + yl
    upper = s >= n_sec // 2
    lower = s < n_sec // 2

    mirror_dev = (n_sec - 1 - s, e, d)
    core_dev = (s, e, d + 1 - 2 * c)

    def peer(dx, f):
        return (s, ((x + dx) % 4) * 2 + (yh + f) % 2, (d + 2 * f) % 4)

    def peer_x(dx, core):
        return (s, ((x + dx) % 4) * 2 + yh, yl * 2 + core)

    def peer_y(dy, core):
        yy = (y + dy) % 4
        return (s, x * 2 + yy // 2, (yy % 2) * 2 + core)

    cp = Copies(send_sems, recv_sems)
    started = []

    def go(copy):
        copy.start()
        started.append(copy)

    closed = []

    def sent(copy):
        copy.wait_send()
        closed.append(copy)

    loads = [
        pltpu.make_async_copy(src, dst, local_sems.at[i])
        for i, (src, dst) in enumerate(
            [(skip_h, skip_v), (down_h, down_v), (gate_h, gate_v), (up_h, up_v)]
        )
    ]
    for load in loads:
        load.start()

    barrier = pltpu.get_barrier_semaphore()
    greeted = [mirror_dev, core_dev]
    greeted += [peer(dx, f) for f in range(2) for dx in range(4) if (dx, f) != (0, 0)]
    greeted += [(s, e, (d + 2) % 4), (s, x * 2 + (yh + 1) % 2, d)]
    greeted += [peer_x(k, 1 - c) for k in (1, 2, 3)] + [peer_y(k, 1 - c) for k in (1, 2, 3)]
    for device in greeted:
        pl.semaphore_signal(barrier, inc=1, device_id=device, device_id_type=MESH)
    pl.semaphore_wait(barrier, len(greeted))

    mirror_in = [cp.make(hid.at[:, pl.ds(j * W, W)], mir.at[j], mirror_dev) for j in range(4)]

    @pl.when(lower)
    def _():
        for copy in mirror_in:
            copy.start()

    def relative(names):
        dx = ((names >> 1) - x + 4) & 3
        f = ((names & 1) - yh + 2) & 1
        label = jnp.zeros_like(names)
        for o, (dx_o, f_o) in enumerate(DISTANCES):
            label = jnp.where((dx == dx_o) & (f == f_o), o, label)
        return label

    lane = lax.broadcasted_iota(jnp.int32, (T, 128), 1)
    row = lax.broadcasted_iota(jnp.int32, (T, 128), 0)
    eye = jnp.where(lane == row, 1.0, 0.0).astype(BF)
    names = dot_rt(eye, ids[...].astype(F32).astype(BF)).astype(jnp.int32)
    id0, id1 = names[:, 0:1], names[:, 1:2]
    rel0, rel1 = relative(id0), relative(id1)
    c0, c1 = rel0 == lane, rel1 == lane
    counts = jnp.where(c0, 1.0, 0.0) + jnp.where(c1, 1.0, 0.0)
    earlier = jnp.where(lane < row, 1.0, 0.0).astype(BF)
    before = dot(earlier, counts.astype(BF))
    rank0 = jnp.sum(jnp.where(c0, before, 0.0), axis=1, keepdims=True)
    rank1 = jnp.sum(jnp.where(c1, before, 0.0), axis=1, keepdims=True)
    slots = lax.broadcasted_iota(jnp.int32, (T, E * CAP), 1).astype(F32)
    at0 = jnp.where(rel0.astype(F32) * CAP + rank0 == slots, 1.0, 0.0)
    at1 = jnp.where(rel1.astype(F32) * CAP + rank1 == slots, 1.0, 0.0)
    a0[...] = at0.astype(BF)
    a1[...] = at1.astype(BF)
    sl[...] = dot_lt((at0 + at1).astype(BF), eye).astype(BF)

    def place(rows, send, recv):
        def tile(i):
            cols = pl.ds(i * W, W)
            placed = dot(sl[...], rows[:, cols]).astype(BF)
            for o in range(E):
                block = placed[o * CAP : (o + 1) * CAP, :]
                if o == 0:
                    recv[0, :, cols] = block
                else:
                    send[o, :, cols] = block

        loop(D // W, tile)

    def dispatch(send, recv, copies, labels):
        for o in labels:
            copies[o] = cp.make(send.at[o], recv.at[o], peer(*DISTANCES[o]))
            go(copies[o])

    def give_back(send, recv, copies, labels):
        for o in labels:
            if o != 0:
                dx, f = DISTANCES[o]
                copies[o] = cp.make(send.at[o], recv.at[o], peer((4 - dx) % 4, f))
                go(copies[o])

    place(cot, gsend, grecv)
    g_cp, n_cp = {}, {}
    dispatch(gsend, grecv, g_cp, [4, 5, 6, 7, 1, 2, 3])

    mine = pl.ds(pl.multiple_of(c * T, T), T)

    def turn(rows, k):
        jto[k // 4, k % 4] = rows.T

    loop(8, lambda k: turn(hid[:, k * T : (k + 1) * T], k))
    ja_early = [cp.make(jto.at[0:2, (y + dy) % 4], ja.at[dy, 0:2, :, mine], peer_y(dy, c)) for dy in (2, 1, 3)]
    ja_late = [cp.make(jto.at[2:4, (y + dy) % 4], ja.at[dy, 2:4, :, mine], peer_y(dy, c)) for dy in (2, 1, 3)]
    jb_all = [((x + dx) % 4, cp.make(jto.at[(x + dx) % 4], jb.at[dx, :, :, mine], peer_x(dx, c))) for dx in (2, 1, 3)]
    loads[0].wait()

    def own_mix(i):
        cols = pl.ds(i * W, W)
        acc[:, cols] = dot(hid[...], skip_v[0:D, cols])

    loop(D // W, own_mix)

    @pl.when(upper)
    def _():
        for j in range(4):
            mirror_in[j].wait_recv()

            def add_mix(i, j=j):
                cols = pl.ds(i * W, W)
                acc[:, cols] += dot(mir[j], skip_v[D + j * W : D + (j + 1) * W, cols])

            loop(D // W, add_mix)

    wide = acc[...].astype(BF).astype(F32)
    acc[...] = wide
    inv_rms = lax.rsqrt(jnp.mean(wide * wide, axis=1, keepdims=True) + norm_eps)
    normed[...] = (wide * inv_rms * gain[...]).astype(BF)

    place(normed, nsend, nrecv)
    dispatch(nsend, nrecv, n_cp, SEND_FIRST)

    lane8 = lax.broadcasted_iota(jnp.int32, (T, 8), 1)
    k0, k1 = id0 == lane8, id1 == lane8
    logits = dot_rt(normed[...], rw[...])
    s0 = jax.nn.sigmoid(jnp.sum(jnp.where(k0, logits, 0.0), axis=1, keepdims=True))
    s1 = jax.nn.sigmoid(jnp.sum(jnp.where(k1, logits, 0.0), axis=1, keepdims=True))
    total = s0 + s1
    w0, w1 = s0 / total, s1 / total

    @pl.when(upper)
    def _():
        loop(8, lambda k: turn(mir[k // 2, :, k % 2 * T : (k % 2 + 1) * T], 8 + k))

    @pl.when(lower)
    def _():
        jto[2:4] = jnp.zeros((2, 4, T, T), BF)

    loads[1].wait()
    for o in g_cp:
        g_cp[o].wait_recv()

    def grad_act(i):
        cols = pl.ds(i * W, W)
        rows = grecv[...].reshape(E * CAP, D)
        ga[:, cols] = dot_rt(rows, down_v[cols, :])

    loop(FF // W, grad_act)

    loads[2].wait()
    loads[3].wait()

    for o in SEND_FIRST:
        sent(n_cp[o])
    dispatch(nsend, nrecv, n_cp, SEND_LAST)

    def split(values, send, recv, cols, labels):
        for k, o in enumerate(labels):
            block = values[k * CAP : (k + 1) * CAP, :]
            if o == 0:
                recv[0, :, cols] = block
            else:
                send[o, :, cols] = block

    o_cp, b_cp, w_cp = {}, {}, {}

    def group(first, last):
        labels = range(first, last)
        count = (last - first) * CAP
        rows = slice(first * CAP, last * CAP)
        for o in labels:
            if o != 0:
                n_cp[o].wait_recv()
        for i in range(FF // W):
            cols = slice(i * W, (i + 1) * W)
            frames = nrecv[first:last].reshape(count, D)
            pre_gate = dot(frames, gate_v[:, cols])
            pre_up = dot(frames, up_v[:, cols])
            grad = ga[rows, cols]
            sig = jax.nn.sigmoid(pre_gate)
            silu = pre_gate * sig
            act[rows, cols] = (silu * pre_up).astype(BF)
            gg[rows, cols] = (grad * pre_up * sig * (1.0 + pre_gate * (1.0 - sig))).astype(BF)
            gu[rows, cols] = (grad * silu).astype(BF)
        if first == 0:
            for copy in ja_early:
                go(copy)
            for xx, copy in jb_all:
                started.append(copy)

                @pl.when(xx < 2)
                def _(copy=copy):
                    copy.start()

        for i in range(D // W):
            cols = slice(i * W, (i + 1) * W)
            grads = dot_rt(gg[rows, :], gate_v[cols, :]) + dot_rt(gu[rows, :], up_v[cols, :])
            split(grads.astype(BF), bsend, brecv, cols, labels)
        give_back(bsend, brecv, b_cp, labels)
        along = 0.0
        for i in range(D // W):
            cols = slice(i * W, (i + 1) * W)
            values = dot(act[rows, :], down_v[:, cols]).astype(BF)
            split(values, osend, orecv, cols, labels)
            grads = grecv[first:last, :, cols].reshape(count, W).astype(F32)
            along += jnp.sum(values.astype(F32) * grads, axis=1, keepdims=True)
        high = along.astype(BF)
        low = (along - high.astype(F32)).astype(BF)
        half = lax.broadcasted_iota(jnp.int32, (count, 128), 1) < 64
        split(jnp.where(half, high, low), wsend, wrecv, slice(0, 128), labels)
        give_back(wsend, wrecv, w_cp, labels)

    for first, last in GROUPS:
        group(first, last)
    for o in b_cp:
        sent(b_cp[o])
    for copy in ja_late:
        go(copy)
    for xx, copy in jb_all:

        @pl.when(xx >= 2)
        def _(copy=copy):
            copy.start()

    give_back(osend, orecv, o_cp, O_FIRST)

    for o in w_cp:
        w_cp[o].wait_recv()
    rows_w = wrecv[...].reshape(E * CAP, 128)
    t0, t1 = dot(a0[...], rows_w), dot(a1[...], rows_w)
    grad_w0 = t0[:, 0:1] + t0[:, 64:65]
    grad_w1 = t1[:, 0:1] + t1[:, 64:65]
    weighted = w0 * grad_w0 + w1 * grad_w1
    gl0 = (grad_w0 - weighted) / total * s0 * (1.0 - s0)
    gl1 = (grad_w1 - weighted) / total * s1 * (1.0 - s1)
    grad_logits = (jnp.where(k0, gl0, 0.0) + jnp.where(k1, gl1, 0.0)).astype(BF)

    for o in b_cp:
        b_cp[o].wait_recv()
    mean_term = 0.0
    for i in range(D // W):
        cols = slice(i * W, (i + 1) * W)
        rows_b = brecv[:, :, cols].reshape(E * CAP, W)
        grad_normed = w0 * dot(a0[...], rows_b) + w1 * dot(a1[...], rows_b)
        grad_normed += dot(grad_logits, rw[:, cols])
        unit = acc[:, cols] * inv_rms
        gain_term = jnp.sum(grad_normed * unit, axis=0, keepdims=True)
        router_term = dot_lt(grad_logits, normed[:, cols])
        both = jnp.concatenate([router_term, jnp.broadcast_to(gain_term, (8, W))], axis=0)
        rgs[i // 2, :, (i % 2) * W : (i % 2 + 1) * W] = both.astype(BF)
        grad_unit = grad_normed * gain[:, cols]
        gn[:, cols] = grad_unit
        mean_term += jnp.sum(grad_unit * unit, axis=1, keepdims=True)
    mean_term = mean_term / D
    rg_1 = [cp.make(rgs.at[1 - c], r1.at[y, c], core_dev)]
    rg_1 += [cp.make(rgs.at[cc], r1.at[y, c], peer_y(dy, cc)) for dy in (2, 1, 3) for cc in (c, 1 - c)]
    for copy in rg_1:
        go(copy)
    r1[y, c] = rgs[c]
    for i in range(D // W):
        cols = slice(i * W, (i + 1) * W)
        unit = acc[:, cols] * inv_rms
        grad_mixed = cot[:, cols].astype(F32) + inv_rms * (gn[:, cols] - unit * mean_term)
        gmq[i] = grad_mixed.astype(BF)
    gm = jnp.concatenate([gmq[0], gmq[1], gmq[2], gmq[3]], axis=1)

    mirror_out = [cp.make(mgs.at[j], mgr.at[j], mirror_dev) for j in range(4)]

    def send_mirror(j):
        mgs[j] = dot_rt(gm, skip_v[D + j * W : D + (j + 1) * W, :]).astype(BF)
        mirror_out[j].start()

    @pl.when(upper)
    def _():
        send_mirror(0)

    gm_a = {0: [cp.make(gmq.at[2 * (1 - c)], ga_x.at[0, mine], core_dev)]}
    gm_b = {0: [cp.make(gmq.at[2 * (1 - c) + 1], gb_x.at[0, mine], core_dev)]}
    for k in (2, 1, 3):
        gm_a[k] = [cp.make(gmq.at[2 * cc], ga_x.at[k, mine], peer_y(k, cc)) for cc in (c, 1 - c)]
        gm_b[k] = [cp.make(gmq.at[2 * cc + 1], gb_x.at[k, mine], peer_x(k, cc)) for cc in (c, 1 - c)]
    for k in (2, 1, 3, 0):
        for copy in gm_a[k] + gm_b[k]:
            go(copy)
    ga_x[0, mine] = gmq[2 * c]
    gb_x[0, mine] = gmq[2 * c + 1]

    @pl.when(upper)
    def _():
        for j in (1, 2, 3):
            send_mirror(j)

    for copy in rg_1:
        copy.wait_recv()
    sum_y = 0.0
    for yy in range(4):
        for cc in range(2):
            sum_y += r1[yy, cc].astype(F32)
    r2[c, x] = sum_y.astype(BF)
    rg_2 = [cp.make(r2.at[c, x], r2.at[c, x], core_dev)]
    rg_2 += [cp.make(r2.at[c, x], r2.at[c, x], peer_x(dx, cc)) for dx in (2, 1, 3) for cc in (c, 1 - c)]
    for copy in rg_2:
        go(copy)

    def own_grad(j):
        cols = pl.ds(j * W, W)
        own_g[:, cols] = dot_rt(gm, skip_v[cols, :]).astype(BF)

    loop(4, own_grad)

    for xx in range(4):
        ja[0, xx, :, mine] = jto[xx, y]
    jb[0, :, :, mine] = jto[x]
    for copy in ja_early + ja_late + [copy for _, copy in jb_all]:
        copy.wait_recv()
    j_core = [cp.make(j.at[:, :, :, mine], j.at[:, :, :, mine], core_dev) for j in (ja, jb)]
    for copy in j_core:
        go(copy)

    for k in range(4):
        for copy in gm_a[k] + gm_b[k]:
            sent(copy)
    give_back(osend, orecv, o_cp, O_LAST)
    for copy in j_core:
        copy.wait_recv()

    def product(frames, grads, copies, parts):
        total = 0.0
        for k in (0, 1, 3, 2):
            for copy in copies[k]:
                copy.wait_recv()
            total += dot(frames[k].reshape(4 * T, 2 * T), grads[k])
        for k in range(4):
            parts[k] = total[k * T : (k + 1) * T, :].astype(BF)

    def pass_on(parts, sums, at, peer_of):
        half = [pl.ds(pl.multiple_of(cc * (T // 2), T // 2), T // 2) for cc in (c, 1 - c)]
        copies = []
        for k in (2, 1, 3):
            for cc, rows in zip((c, 1 - c), half):
                copies.append(cp.make(parts.at[(at + k) % 4, rows], sums.at[c, k], peer_of(k, cc)))
        copies.append(cp.make(parts.at[at, half[1]], sums.at[c, 0], core_dev))
        for copy in copies:
            go(copy)
        sums[c, 0] = parts[at, half[0]]
        return copies

    product(ja, ga_x, gm_a, pa)
    ra_cp = pass_on(pa, ra, x, peer_x)
    product(jb, gb_x, gm_b, pb)
    rb_cp = pass_on(pb, rb, y, peer_y)

    for o in o_cp:
        o_cp[o].wait_recv()
    for i in range(D // W):
        cols = slice(i * W, (i + 1) * W)
        rows_o = orecv[:, :, cols].reshape(E * CAP, W)
        p0, p1 = dot(a0[...], rows_o), dot(a1[...], rows_o)
        out_o[:, cols] = (acc[:, cols] + w0 * p0 + w1 * p1).astype(BF)

    for copy in rg_2:
        copy.wait_recv()
    for h in range(2):
        cols = slice(h * H, (h + 1) * H)
        sums = 0.0
        for xx in range(4):
            sums += r2[h, xx].astype(F32)
        rg_o[:, cols] = sums[0:8, :]
        gg_o[:, cols] = sums[8:9, :]

    for copy in ra_cp + rb_cp:
        copy.wait_recv()
    for cc in range(2):
        for part, start in ((ra, cc * H), (rb, cc * H + W)):
            sums = 0.0
            for k in range(4):
                sums += part[cc, k].astype(F32)
            sg_o[:, start : start + W] = sums

    @pl.when(upper)
    def _():
        hg_o[...] = own_g[...]

    @pl.when(lower)
    def _():
        for j in range(4):
            mirror_out[j].wait_recv()
            cols = slice(j * W, (j + 1) * W)
            hg_o[:, cols] = (own_g[:, cols].astype(F32) + mgr[j].astype(F32)).astype(BF)

    for copy in started:
        if not any(copy is other for other in closed):
            copy.wait_send()

    @pl.when(lower)
    def _():
        for copy in mirror_in:
            copy.wait_send()

    @pl.when(upper)
    def _():
        for copy in mirror_out:
            copy.wait_send()


def hand_on(*refs):
    for source, target in zip(refs[:5], refs[5:]):
        target[...] = source[...]


def per_device(
    hidden, expert_ids, cotangent, skip_weight, norm_gain, router_weight,
    gate_weight, up_weight, down_weight,
):
    T, D = hidden.shape[1:]
    FF = gate_weight.shape[-1]
    E = lax.axis_size("expert")
    CAP = min(T, 3 * T // E)
    W, H = D // 4, D // 2
    slots = E * CAP
    vmem = pl.BlockSpec(memory_space=pltpu.VMEM)
    anywhere = pl.BlockSpec(memory_space=pl.ANY)
    a2a = pltpu.VMEM((E, CAP, D), BF)
    scratch = [
        pltpu.VMEM((2 * D, D), BF), pltpu.VMEM((D, FF), BF), pltpu.VMEM((D, FF), BF), pltpu.VMEM((FF, D), BF),
        pltpu.VMEM((4, T, W), BF), pltpu.VMEM((4, 4, T, T), BF), pltpu.VMEM((4, 4, T, 2 * T), BF), pltpu.VMEM((4, 4, T, 2 * T), BF),
        pltpu.VMEM((T, slots), BF), pltpu.VMEM((T, slots), BF), pltpu.VMEM((slots, T), BF),
        a2a, a2a, a2a, a2a, a2a, a2a, a2a, a2a, pltpu.VMEM((E, CAP, 128), BF), pltpu.VMEM((E, CAP, 128), BF),
        pltpu.VMEM((slots, FF), F32), pltpu.VMEM((slots, FF), BF), pltpu.VMEM((slots, FF), BF), pltpu.VMEM((slots, FF), BF),
        pltpu.VMEM((T, D), F32), pltpu.VMEM((T, D), BF), pltpu.VMEM((T, D), F32),
        pltpu.VMEM((2, 16, H), BF), pltpu.VMEM((4, 2, 16, H), BF), pltpu.VMEM((2, 4, 16, H), BF),
        pltpu.VMEM((4, T, W), BF), pltpu.VMEM((4, 2 * T, W), BF), pltpu.VMEM((4, 2 * T, W), BF),
        pltpu.VMEM((4, T, W), BF), pltpu.VMEM((4, T, W), BF), pltpu.VMEM((T, D), BF),
        pltpu.VMEM((4, T, W), BF), pltpu.VMEM((4, T, W), BF), pltpu.VMEM((2, 4, T // 2, W), BF), pltpu.VMEM((2, 4, T // 2, W), BF),
        pltpu.SemaphoreType.DMA((4,)), pltpu.SemaphoreType.DMA((N_SEM,)), pltpu.SemaphoreType.DMA((N_SEM,)),
    ]
    results = pl.pallas_call(
        kernel,
        out_shape=(
            jax.ShapeDtypeStruct((T, D), BF),
            jax.ShapeDtypeStruct((T, D), BF),
            jax.ShapeDtypeStruct((T // 2, D), F32),
            jax.ShapeDtypeStruct((8, D), F32),
            jax.ShapeDtypeStruct((1, D), F32),
        ),
        in_specs=[vmem] * 5 + [anywhere] * 4,
        out_specs=[vmem] * 5,
        scratch_shapes=scratch,
        compiler_params=pltpu.CompilerParams(
            collective_id=0, has_side_effects=True, vmem_limit_bytes=60 * 1024 * 1024
        ),
    )(
        hidden[0], expert_ids[0].T, cotangent[0], norm_gain, router_weight[0].T,
        skip_weight[0], gate_weight[0, 0], up_weight[0, 0], down_weight[0, 0],
    )
    out, hidden_grad, skip_grad, router, gain = pl.pallas_call(
        hand_on,
        out_shape=tuple(jax.ShapeDtypeStruct(r.shape, r.dtype) for r in results),
        in_specs=[vmem] * 5,
        out_specs=[vmem] * 5,
    )(*results)
    return (out[None], hidden_grad[None], skip_grad[None], router.T[None], gain)


def solution(mesh):
    return jax.shard_map(
        per_device,
        mesh=mesh,
        in_specs=(
            P("section", ("expert", "dp"), None),
            P("section", ("expert", "dp"), None),
            P("section", ("expert", "dp"), None),
            P("section", None, None),
            P("section", None),
            P("section", None, None),
            P("section", "expert", None, None),
            P("section", "expert", None, None),
            P("section", "expert", None, None),
        ),
        out_specs=(
            P("section", ("expert", "dp"), None),
            P("section", ("expert", "dp"), None),
            P("section", ("expert", "dp"), None),
            P("section", None, None),
            P("section", None),
        ),
        check_vma=False,
    )
```

time: 83.9 us -> 76.9 us (0.917)
  Pallas kernels: 83.1 us -> 76.2 us
    pallas_call x1, Pallas kernels: 81.1 us -> 74.1 us  [per_device(): pl.pallas_call(kernel, out_shape=(jax.ShapeDtypeStruct((T, D), BF), jax.S...]
where the time goes in v3:
time: 76.9 us; the launch traced here: 76.8 us
  Pallas kernels  76.2 us (99%)
    pallas_call x1, Pallas kernels, per_device(): pl.pallas_call(kernel, out_shape=(jax.ShapeDtypeStruct((T, D), BF), jax.S...  74.1 us
    pallas_call x1, Pallas kernels, per_device(): pl.pallas_call(hand_on, out_shape=tuple((jax.ShapeDtypeStruct(r.shape, r....  2.04 us

profile of v3, /device:TPU:1, one launch (start us, length us, event | category | flops | bytes accessed | tf_op | source)
XLA Modules:
  0.0 76.8 jit_solution(8733664213310780044)
XLA Ops:
  0.6 74.1 %shard_map.128 = (bf16[128,1024]{1,0:T(8,128)(2,1)}, bf16[128,1024]{1,0:T(8,128)(2,1)}, f32[64,1024]{1,0:T(8,128)}, f32[8,1024]{1,0:T(8,128)}, f32[1,1024]{1,0:T(1,128)}) custom-call(bf16[128,1024]{1,0:T(8,128)(2,1)} %bitcast.22, s32[2,128]{1,0:T(2,128)} %bitcast.25, bf16[128,1024]{1,0:T(8,128)(2,1)} %bitcast.23, f32[1,1024]{1,0:T(1,128)} %gain.1, ...), custom_call_target="tpu_custom_call" | custom-call | tf_op jit(solution)/shard_map/pallas_call | solution.py:546
  74.8 2.0 %shard_map.129 = (bf16[128,1024]{1,0:T(8,128)(2,1)}, bf16[128,1024]{1,0:T(8,128)(2,1)}, f32[64,1024]{1,0:T(8,128)}, f32[8,1024]{1,0:T(8,128)}, f32[1,1024]{1,0:T(1,128)}) custom-call(bf16[128,1024]{1,0:T(8,128)(2,1)} %get-tuple-element.15.refs_0_, bf16[128,1024]{1,0:T(8,128)(2,1)} %get-tuple-element.16.refs_1_, f32[64,1024]{1,0:T(8,128)} %get-tuple-element.17.refs_2_, ...), custom_call_target="tpu_custom_call" | custom-call | tf_op jit(solution)/shard_map/pallas_call | solution.py:565

commit v4 on v3

--- a/solution.py
+++ b/solution.py
@@ -51,7 +51,7 @@
 DISTANCES = [(0, 0), (1, 0), (3, 0), (0, 1), (2, 1), (2, 0), (1, 1), (3, 1)]
 GROUPS = [(0, 5), (5, 8)]
 SEND_FIRST, SEND_LAST = [4, 3, 1, 2], [6, 7, 5]
-O_FIRST, O_LAST = [3, 1, 2], [4, 6, 7, 5]
+O_FIRST, O_LAST = [4, 6, 5], [7, 3, 1, 2]
 
 
 def kernel(
@@ -128,14 +128,6 @@
     greeted += [peer_x(k, 1 - c) for k in (1, 2, 3)] + [peer_y(k, 1 - c) for k in (1, 2, 3)]
     for device in greeted:
         pl.semaphore_signal(barrier, inc=1, device_id=device, device_id_type=MESH)
-    pl.semaphore_wait(barrier, len(greeted))
-
-    mirror_in = [cp.make(hid.at[:, pl.ds(j * W, W)], mir.at[j], mirror_dev) for j in range(4)]
-
-    @pl.when(lower)
-    def _():
-        for copy in mirror_in:
-            copy.start()
 
     def relative(names):
         dx = ((names >> 1) - x + 4) & 3
@@ -190,6 +182,15 @@
                 go(copies[o])
 
     place(cot, gsend, grecv)
+    pl.semaphore_wait(barrier, len(greeted))
+
+    mirror_in = [cp.make(hid.at[:, pl.ds(j * W, W)], mir.at[j], mirror_dev) for j in range(4)]
+
+    @pl.when(lower)
+    def _():
+        for copy in mirror_in:
+            copy.start()
+
     g_cp, n_cp = {}, {}
     dispatch(gsend, grecv, g_cp, [4, 5, 6, 7, 1, 2, 3])
 
@@ -262,6 +263,8 @@
     for o in SEND_FIRST:
         sent(n_cp[o])
     dispatch(nsend, nrecv, n_cp, SEND_LAST)
+    for copy in ja_early:
+        go(copy)
 
     def split(values, send, recv, cols, labels):
         for k, o in enumerate(labels):
@@ -291,21 +294,15 @@
             act[rows, cols] = (silu * pre_up).astype(BF)
             gg[rows, cols] = (grad * pre_up * sig * (1.0 + pre_gate * (1.0 - sig))).astype(BF)
             gu[rows, cols] = (grad * silu).astype(BF)
-        if first == 0:
-            for copy in ja_early:
-                go(copy)
-            for xx, copy in jb_all:
-                started.append(copy)
-
-                @pl.when(xx < 2)
-                def _(copy=copy):
-                    copy.start()
-
         for i in range(D // W):
             cols = slice(i * W, (i + 1) * W)
             grads = dot_rt(gg[rows, :], gate_v[cols, :]) + dot_rt(gu[rows, :], up_v[cols, :])
             split(grads.astype(BF), bsend, brecv, cols, labels)
         give_back(bsend, brecv, b_cp, labels)
+    def group_outputs(first, last):
+        labels = range(first, last)
+        count = (last - first) * CAP
+        rows = slice(first * CAP, last * CAP)
         along = 0.0
         for i in range(D // W):
             cols = slice(i * W, (i + 1) * W)
@@ -321,17 +318,12 @@
 
     for first, last in GROUPS:
         group(first, last)
+    for first, last in GROUPS:
+        group_outputs(first, last)
     for o in b_cp:
         sent(b_cp[o])
-    for copy in ja_late:
+    for copy in ja_late + [copy for _, copy in jb_all]:
         go(copy)
-    for xx, copy in jb_all:
-
-        @pl.when(xx >= 2)
-        def _(copy=copy):
-            copy.start()
-
-    give_back(osend, orecv, o_cp, O_FIRST)
 
     for o in w_cp:
         w_cp[o].wait_recv()
@@ -399,6 +391,8 @@
         for j in (1, 2, 3):
             send_mirror(j)
 
+    give_back(osend, orecv, o_cp, O_FIRST)
+
     for copy in rg_1:
         copy.wait_recv()
     sum_y = 0.0
@@ -426,9 +420,6 @@
     for copy in j_core:
         go(copy)
 
-    for k in range(4):
-        for copy in gm_a[k] + gm_b[k]:
-            sent(copy)
     give_back(osend, orecv, o_cp, O_LAST)
     for copy in j_core:
         copy.wait_recv()

time: 76.9 us -> 73.3 us (0.953)
  the two profiles are of different devices: /device:TPU:1 before, /device:TPU:129 now
where the time goes in v4:
time: 73.3 us; the launch traced here: 73.2 us
  Pallas kernels  72.5 us (99%)
    pallas_call x1, Pallas kernels, per_device(): pl.pallas_call(kernel, out_shape=(jax.ShapeDtypeStruct((T, D), BF), jax.S...  70.5 us
    pallas_call x1, Pallas kernels, per_device(): pl.pallas_call(hand_on, out_shape=tuple((jax.ShapeDtypeStruct(r.shape, r....  2.04 us

profile of v4, /device:TPU:129, one launch (start us, length us, event | category | flops | bytes accessed | tf_op | source)
XLA Modules:
  0.0 73.2 jit_solution(15096171435633743926)
XLA Ops:
  0.6 70.5 %shard_map.128 = (bf16[128,1024]{1,0:T(8,128)(2,1)}, bf16[128,1024]{1,0:T(8,128)(2,1)}, f32[64,1024]{1,0:T(8,128)}, f32[8,1024]{1,0:T(8,128)}, f32[1,1024]{1,0:T(1,128)}) custom-call(bf16[128,1024]{1,0:T(8,128)(2,1)} %bitcast.22, s32[2,128]{1,0:T(2,128)} %bitcast.25, bf16[128,1024]{1,0:T(8,128)(2,1)} %bitcast.23, f32[1,1024]{1,0:T(1,128)} %gain.1, ...), custom_call_target="tpu_custom_call" | custom-call | tf_op jit(solution)/shard_map/pallas_call | solution.py:537
  71.1 2.0 %shard_map.129 = (bf16[128,1024]{1,0:T(8,128)(2,1)}, bf16[128,1024]{1,0:T(8,128)(2,1)}, f32[64,1024]{1,0:T(8,128)}, f32[8,1024]{1,0:T(8,128)}, f32[1,1024]{1,0:T(1,128)}) custom-call(bf16[128,1024]{1,0:T(8,128)(2,1)} %get-tuple-element.15.refs_0_, bf16[128,1024]{1,0:T(8,128)(2,1)} %get-tuple-element.16.refs_1_, f32[64,1024]{1,0:T(8,128)} %get-tuple-element.17.refs_2_, ...), custom_call_target="tpu_custom_call" | custom-call | tf_op jit(solution)/shard_map/pallas_call | solution.py:556

commit v5 on v4

--- a/solution.py
+++ b/solution.py
@@ -263,8 +263,6 @@
     for o in SEND_FIRST:
         sent(n_cp[o])
     dispatch(nsend, nrecv, n_cp, SEND_LAST)
-    for copy in ja_early:
-        go(copy)
 
     def split(values, send, recv, cols, labels):
         for k, o in enumerate(labels):
@@ -322,7 +320,7 @@
         group_outputs(first, last)
     for o in b_cp:
         sent(b_cp[o])
-    for copy in ja_late + [copy for _, copy in jb_all]:
+    for copy in ja_early + ja_late + [copy for _, copy in jb_all]:
         go(copy)
 
     for o in w_cp:

time: 73.3 us -> 72 us (0.982)
  the two profiles are of different devices: /device:TPU:129 before, /device:TPU:1 now
where the time goes in v5:
time: 72 us; the launch traced here: 70.8 us
  Pallas kernels  70.1 us (97%)
    pallas_call x1, Pallas kernels, per_device(): pl.pallas_call(kernel, out_shape=(jax.ShapeDtypeStruct((T, D), BF), jax.S...  68.1 us
    pallas_call x1, Pallas kernels, per_device(): pl.pallas_call(hand_on, out_shape=tuple((jax.ShapeDtypeStruct(r.shape, r....  2.04 us

profile of v5, /device:TPU:1, one launch (start us, length us, event | category | flops | bytes accessed | tf_op | source)
XLA Modules:
  0.0 70.8 jit_solution(9393670904618687106)
XLA Ops:
  0.6 68.1 %shard_map.128 = (bf16[128,1024]{1,0:T(8,128)(2,1)}, bf16[128,1024]{1,0:T(8,128)(2,1)}, f32[64,1024]{1,0:T(8,128)}, f32[8,1024]{1,0:T(8,128)}, f32[1,1024]{1,0:T(1,128)}) custom-call(bf16[128,1024]{1,0:T(8,128)(2,1)} %bitcast.22, s32[2,128]{1,0:T(2,128)} %bitcast.25, bf16[128,1024]{1,0:T(8,128)(2,1)} %bitcast.23, f32[1,1024]{1,0:T(1,128)} %gain.1, ...), custom_call_target="tpu_custom_call" | custom-call | tf_op jit(solution)/shard_map/pallas_call | solution.py:535
  68.7 2.0 %shard_map.129 = (bf16[128,1024]{1,0:T(8,128)(2,1)}, bf16[128,1024]{1,0:T(8,128)(2,1)}, f32[64,1024]{1,0:T(8,128)}, f32[8,1024]{1,0:T(8,128)}, f32[1,1024]{1,0:T(1,128)}) custom-call(bf16[128,1024]{1,0:T(8,128)(2,1)} %get-tuple-element.15.refs_0_, bf16[128,1024]{1,0:T(8,128)(2,1)} %get-tuple-element.16.refs_1_, f32[64,1024]{1,0:T(8,128)} %get-tuple-element.17.refs_2_, ...), custom_call_target="tpu_custom_call" | custom-call | tf_op jit(solution)/shard_map/pallas_call | solution.py:554
